TPU v7x, 32 devices: a whole 2x2x4 slice. The times are simulated.
32 devices in a mesh: dp: 4 (over y, core), row: 4 (over z), col: 2 (over x).
Axes of the slice: x: 2, y: 2, z: 4, core: 2. Of those that a mesh axis runs over, the one named last changes fastest.
Arguments:
- tokens: bfloat16 [4096, 2048], P(('dp', 'row', 'col')), may hold values from -6 to 6
- cotangent: bfloat16 [4096, 2048], P(('dp', 'row', 'col')), may hold values from -6 to 6
- w_query: bfloat16 [2048, 2048], P(('dp', 'row', 'col')), may hold values from -0.125 to 0.125
- w_keyval: bfloat16 [2048, 256], P(('dp', 'row', 'col')), may hold values from -0.125 to 0.125
- w_out: bfloat16 [2048, 2048], P(('dp', 'row', 'col')), may hold values from -1 to 1
- norm_attn: bfloat16 [2048], P(('dp', 'row', 'col')), may hold values from 0.25 to 1.75
- norm_ffn: bfloat16 [2048], P(('dp', 'row', 'col')), may hold values from 0.25 to 1.75
- w_gate: bfloat16 [2048, 6144], P('col', 'row'), may hold values from -0.125 to 0.125
- w_up: bfloat16 [2048, 6144], P('col', 'row'), may hold values from -0.125 to 0.125
- w_down: bfloat16 [6144, 2048], P('row', 'col'), may hold values from -0.078125 to 0.078125
- lengths: int32 [4, 4], P('dp'), may hold values from 1 to 512, 960 in all within a row
- placement: int32 [4, 4], P('dp'), may hold values from 0 to 3, each once within a row
Outputs:
- result: bfloat16 [4096, 2048], P(('dp', 'row'), 'col')
- grad_tokens: bfloat16 [4096, 2048], P(('dp', 'row', 'col'))
- grad_query: float32 [2048, 2048], P(('dp', 'row', 'col'))
- grad_keyval: float32 [2048, 256], P(('dp', 'row', 'col'))
- grad_out: float32 [2048, 2048], P(('dp', 'row', 'col'))
- grad_norm_attn: float32 [2048], P(('dp', 'row', 'col'))
- grad_norm_ffn: float32 [2048], P(('dp', 'row', 'col'))
- grad_gate: float32 [2048, 6144], P('col', 'row')
- grad_up: float32 [2048, 6144], P('col', 'row')
- grad_down: float32 [6144, 2048], P('row', 'col')
Inputs may be any that keep to these rules, and one draw needn't show every extreme that they name: In each row the 4 lengths sum to 960, and the largest is exactly 512. `placement`: each row names every sequence of its group once.
All inputs are finite; a program needn't handle non-finite values.
Results may differ from a plain program's by a relative error of at most 0.019.
Values may be sent and summed in bfloat16 or wider, within the bound.
No kernel may reach another device: no remote copies, remote signals or barrier semaphores. Data moves between devices by JAX's collectives and lax.ppermute only.
A program may use at most 192 MiB of HBM per device.

v0:
```python
import math

import jax
import jax.numpy as jnp
from jax import lax
from jax.sharding import PartitionSpec as P

HEADS = 16
HEAD = 128
WINDOW = 1024


EPSILON = 1e-06
ROPE_BASE = 10000.0
NEG_FILL = -1e30


def from_behind(array, axis, by):
    size = lax.axis_size(axis)
    pairs = [(i, i + by) for i in range(size) if 0 <= i + by < size]
    return lax.ppermute(array, axis, pairs)


def rms_norm(values, gain_vec):
    return (
        values * lax.rsqrt(jnp.mean(values * values, axis=-1, keepdims=True) + EPSILON) * gain_vec
    )


def rotate(values, offset):
    half_width = values.shape[-1] // 2
    frequency = ROPE_BASE ** (-2.0 * jnp.arange(half_width, dtype=jnp.float32) / values.shape[-1])
    angles = offset.astype(jnp.float32)[:, None] * frequency[None, :]
    angles = angles.reshape((values.shape[0],) + (1,) * (values.ndim - 2) + (half_width,))
    cos_part = jnp.cos(angles)
    sin_part = jnp.sin(angles)
    lower_half = values[..., :half_width]
    upper_half = values[..., half_width:]
    return jnp.concatenate(
        [
            lower_half * cos_part - upper_half * sin_part,
            upper_half * cos_part + lower_half * sin_part,
        ],
        axis=-1,
    )


def token_layout(length_row, order_row, first_row, row_count):
    seq_count = length_row.shape[0]
    slot_ids = jnp.arange(seq_count, dtype=jnp.int32)
    placed = jnp.sum(
        jnp.where(order_row[:, None] == slot_ids[None, :], length_row[None, :], 0),
        axis=1,
        dtype=jnp.int32,
    )
    seq_ends = jnp.cumsum(placed, dtype=jnp.int32)
    starts = seq_ends - placed
    where_at = first_row + jnp.arange(row_count, dtype=jnp.int32)
    slot_of = jnp.sum(
        (where_at[:, None] >= seq_ends[None, :]).astype(jnp.int32), axis=1, dtype=jnp.int32
    )
    seq_begin = jnp.sum(
        jnp.where(slot_of[:, None] == slot_ids[None, :], starts[None, :], 0),
        axis=1,
        dtype=jnp.int32,
    )
    inside = slot_of < seq_count
    segment = jnp.where(inside, slot_of, seq_count + where_at)
    segment = jnp.where(where_at < 0, -1, segment)
    offset = jnp.where(inside, where_at - seq_begin, 0)
    return (segment, where_at, offset)


def plain_dot(left_side, right_side):
    return jnp.dot(left_side, right_side, preferred_element_type=jnp.float32)


def inner_rows(left_side, right_side):
    return lax.dot_general(
        left_side, right_side, (((0,), (0,)), ((), ())), preferred_element_type=jnp.float32
    )


def inner_cols(left_side, right_side):
    return lax.dot_general(
        left_side, right_side, (((1,), (1,)), ((), ())), preferred_element_type=jnp.float32
    )


def column_gather(values):
    return lax.all_gather(values, "col", axis=0, tiled=True)


def column_sum(term_fn, row_count):
    return lax.psum_scatter(
        term_fn(jnp.int32(0), row_count * lax.axis_size("col")),
        "col",
        scatter_dimension=0,
        tiled=True,
    )


def row_sum(term_fn, row_count):
    return lax.psum_scatter(
        term_fn(jnp.int32(0), row_count * lax.axis_size("row")),
        "row",
        scatter_dimension=0,
        tiled=True,
    )


def forward_pass(
    tokens,
    cotangent,
    w_query,
    w_keyval,
    w_out,
    norm_attn,
    norm_ffn,
    w_gate,
    w_up,
    lengths,
    placement,
):
    full_query, full_keyval, full_out, gain_attn, gain_ffn = (
        lax.all_gather(w_query, ("dp", "row", "col"), axis=0, tiled=True),
        lax.all_gather(w_keyval, ("dp", "row", "col"), axis=0, tiled=True),
        lax.all_gather(w_out, ("dp", "row", "col"), axis=0, tiled=True),
        lax.all_gather(norm_attn, ("dp", "row", "col"), axis=0, tiled=True),
        lax.all_gather(norm_ffn, ("dp", "row", "col"), axis=0, tiled=True),
    )
    gain_attn = gain_attn.astype(jnp.float32)
    gain_ffn = gain_ffn.astype(jnp.float32)
    row_count = tokens.shape[0]
    first_row = lax.axis_index(("row", "col")) * row_count
    reach_back = min(lax.axis_size(("row", "col")) - 1, (WINDOW - 2 + row_count) // row_count)
    segment, where_at, offset = token_layout(lengths[0], placement[0], first_row, row_count)
    key_segment, key_at, unused_offset = token_layout(
        lengths[0], placement[0], first_row - reach_back * row_count, (reach_back + 1) * row_count
    )
    allowed = (key_segment[None, :] == segment[:, None]) & (key_at[None, :] <= where_at[:, None])
    inputs = tokens.astype(jnp.float32)
    attn_in = rms_norm(inputs, gain_attn).astype(jnp.bfloat16)
    query_raw = plain_dot(attn_in, full_query)
    keyval_raw = plain_dot(attn_in, full_keyval)
    score_scale = 1.0 / math.sqrt(HEAD)
    query_low = (rotate(query_raw.reshape(row_count, HEADS, HEAD), offset) * score_scale).astype(
        jnp.bfloat16
    )
    keyval_low = jnp.concatenate(
        [rotate(keyval_raw[:, :HEAD], offset), keyval_raw[:, HEAD:]], axis=1
    ).astype(jnp.bfloat16)

    def pass_on(carried, unused):
        arrived = from_behind(carried, ("row", "col"), 1)
        return (arrived, arrived)

    unused_last, earlier = lax.scan(pass_on, keyval_low, None, length=reach_back)
    key_rows = jnp.concatenate(
        [earlier[::-1].reshape(reach_back * row_count, 2 * HEAD), keyval_low], axis=0
    )
    scores = jnp.einsum(
        "qhd,kd->hqk", query_low, key_rows[:, :HEAD], preferred_element_type=jnp.float32
    )
    masked = jnp.where(allowed[None], scores, NEG_FILL)
    row_peak = jnp.max(masked, axis=-1, keepdims=True)
    expo_vals = jnp.where(allowed[None], jnp.exp(masked - row_peak), 0.0)
    expo_sum = jnp.sum(expo_vals, axis=-1, keepdims=True)
    log_total = row_peak + jnp.log(expo_sum)
    weights_low = (expo_vals / expo_sum).astype(jnp.bfloat16)
    mixed = jnp.einsum(
        "hqk,kd->qhd", weights_low, key_rows[:, HEAD:], preferred_element_type=jnp.float32
    )
    mixed_low = mixed.reshape(row_count, HEADS * HEAD).astype(jnp.bfloat16)
    branch = plain_dot(mixed_low, full_out).astype(jnp.bfloat16)
    residual = inputs + branch.astype(jnp.float32)
    ffn_in = rms_norm(residual, gain_ffn).astype(jnp.bfloat16)
    x_rows, branch_rows, ffn_rows, cot_rows = (
        lax.all_to_all(tokens, "col", split_axis=1, concat_axis=0, tiled=True),
        lax.all_to_all(branch, "col", split_axis=1, concat_axis=0, tiled=True),
        lax.all_to_all(ffn_in, "col", split_axis=1, concat_axis=0, tiled=True),
        lax.all_to_all(cotangent, "col", split_axis=1, concat_axis=0, tiled=True),
    )
    ffn_all, cot_all = (
        lax.all_gather(ffn_rows, "row", axis=0, tiled=True),
        lax.all_gather(cot_rows, "row", axis=0, tiled=True),
    )
    both_in = jnp.concatenate([w_gate, w_up], axis=1)

    def project_in(row_start, piece_rows):
        return plain_dot(ffn_all, both_in)

    gate_up = column_sum(project_in, ffn_all.shape[0] // lax.axis_size("col"))
    ffn_width = w_gate.shape[1]
    gate_act = gate_up[:, :ffn_width]
    up_act = gate_up[:, ffn_width:]
    hidden_low = (jax.nn.gelu(gate_act, approximate=True) * up_act).astype(jnp.bfloat16)
    hidden_all = column_gather(hidden_low)
    return (
        inputs,
        gain_attn,
        gain_ffn,
        full_query,
        full_keyval,
        full_out,
        offset,
        allowed,
        attn_in,
        query_raw,
        keyval_raw,
        query_low,
        key_rows,
        log_total,
        mixed_low,
        residual,
        x_rows,
        branch_rows,
        ffn_all,
        cot_all,
        both_in,
        gate_act,
        up_act,
        hidden_all,
        reach_back,
    )


def shards(
    tokens,
    cotangent,
    w_query,
    w_keyval,
    w_out,
    norm_attn,
    norm_ffn,
    w_gate,
    w_up,
    w_down,
    lengths,
    placement,
):
    stored = forward_pass(
        tokens,
        cotangent,
        w_query,
        w_keyval,
        w_out,
        norm_attn,
        norm_ffn,
        w_gate,
        w_up,
        lengths,
        placement,
    )
    hidden_first = stored[23]
    x_first = stored[16]
    branch_first = stored[17]

    def project_out(row_start, piece_rows):
        return plain_dot(hidden_first, w_down)

    ffn_out = row_sum(project_out, x_first.shape[0])
    result = (x_first.astype(jnp.float32) + branch_first.astype(jnp.float32) + ffn_out).astype(
        jnp.bfloat16
    )
    redone = lax.optimization_barrier(
        (
            tokens,
            cotangent,
            w_query,
            w_keyval,
            w_out,
            norm_attn,
            norm_ffn,
            w_gate,
            w_up,
            w_down,
            lengths,
            placement,
            result,
        )
    )
    stored = forward_pass(
        redone[0],
        redone[1],
        redone[2],
        redone[3],
        redone[4],
        redone[5],
        redone[6],
        redone[7],
        redone[8],
        redone[10],
        redone[11],
    )
    (
        inputs,
        gain_attn,
        gain_ffn,
        full_query,
        full_keyval,
        full_out,
        offset,
        allowed,
        attn_in,
        query_raw,
        keyval_raw,
        query_low,
        key_rows,
        log_total,
        mixed_low,
        residual,
        x_rows,
        branch_rows,
        ffn_all,
        cot_all,
        both_in,
        gate_act,
        up_act,
        hidden_all,
        reach_back,
    ) = stored
    row_count = inputs.shape[0]
    ffn_width = w_gate.shape[1]

    def back_hidden(row_start, piece_rows):
        return inner_cols(cot_all, w_down)

    hidden_grad = column_sum(back_hidden, gate_act.shape[0])

    def glu_part(gate_in, up_in):
        return jax.nn.gelu(gate_in, approximate=True) * up_in

    unused_glu, glu_back = jax.vjp(glu_part, gate_act, up_act)
    gate_grad, up_grad = glu_back(hidden_grad)
    gate_up_grad = jnp.concatenate([gate_grad, up_grad], axis=1).astype(jnp.bfloat16)
    grad_down = inner_rows(hidden_all, cot_all)
    grads_all = column_gather(gate_up_grad)
    grad_both = inner_rows(ffn_all, grads_all)

    def back_in(row_start, piece_rows):
        return inner_cols(grads_all, both_in)

    ffn_grad = row_sum(back_in, x_rows.shape[0]).astype(jnp.bfloat16)
    ffn_grad_tok = lax.all_to_all(ffn_grad, "col", split_axis=0, concat_axis=1, tiled=True)
    unused_second, second_back = jax.vjp(rms_norm, residual, gain_ffn)
    resid_part, gain_ffn_grad = second_back(ffn_grad_tok.astype(jnp.float32))
    resid_grad = cotangent.astype(jnp.float32) + resid_part
    branch_grad = resid_grad.astype(jnp.bfloat16)
    grad_out = inner_rows(mixed_low, branch_grad)
    mixed_grad = (
        inner_cols(branch_grad, full_out).astype(jnp.bfloat16).reshape(row_count, HEADS, HEAD)
    )
    scores = jnp.einsum(
        "qhd,kd->hqk", query_low, key_rows[:, :HEAD], preferred_element_type=jnp.float32
    )
    weights_f = jnp.exp(jnp.where(allowed[None], scores - log_total, NEG_FILL))
    weights_low = weights_f.astype(jnp.bfloat16)
    value_dir = jnp.einsum(
        "qhd,kd->hqk", mixed_grad, key_rows[:, HEAD:], preferred_element_type=jnp.float32
    )
    score_grad = weights_f * (value_dir - jnp.sum(weights_f * value_dir, axis=-1, keepdims=True))
    score_low = score_grad.astype(jnp.bfloat16)
    query_grad = jnp.einsum(
        "hqk,kd->qhd", score_low, key_rows[:, :HEAD], preferred_element_type=jnp.float32
    )
    key_grad = jnp.einsum("hqk,qhd->kd", score_low, query_low, preferred_element_type=jnp.float32)
    value_grad = jnp.einsum(
        "hqk,qhd->kd", weights_low, mixed_grad, preferred_element_type=jnp.float32
    )
    keyval_grad = jnp.concatenate([key_grad, value_grad], axis=1).reshape(
        reach_back + 1, row_count, 2 * HEAD
    )
    ordered = keyval_grad[::-1]

    def pass_back(carried, piece_in):
        return (
            from_behind(carried.astype(jnp.bfloat16), ("row", "col"), -1).astype(carried.dtype)
            + piece_in,
            None,
        )

    keyval_total, unused_scan = lax.scan(pass_back, ordered[reach_back], ordered[:reach_back][::-1])

    def rotate_keys(raw_rows):
        return jnp.concatenate([rotate(raw_rows[:, :HEAD], offset), raw_rows[:, HEAD:]], axis=1)

    unused_keys, keys_back = jax.vjp(rotate_keys, keyval_raw)
    keyval_low_grad = keys_back(keyval_total)[0].astype(jnp.bfloat16)
    score_scale = 1.0 / math.sqrt(HEAD)

    def rotate_query(raw_rows):
        return rotate(raw_rows.reshape(row_count, HEADS, HEAD), offset) * score_scale

    unused_query, query_back = jax.vjp(rotate_query, query_raw)
    query_low_grad = query_back(query_grad)[0].astype(jnp.bfloat16)
    attn_in_grad = inner_cols(query_low_grad, full_query) + inner_cols(keyval_low_grad, full_keyval)
    grad_query = inner_rows(attn_in, query_low_grad)
    grad_keyval = inner_rows(attn_in, keyval_low_grad)
    unused_first, first_back = jax.vjp(rms_norm, inputs, gain_attn)
    input_part, gain_attn_grad = first_back(attn_in_grad)
    tokens_grad = (resid_grad + input_part).astype(jnp.bfloat16)
    grad_sums = (
        lax.psum_scatter(grad_query, ("dp", "row", "col"), scatter_dimension=0, tiled=True),
        lax.psum_scatter(grad_keyval, ("dp", "row", "col"), scatter_dimension=0, tiled=True),
        lax.psum_scatter(grad_out, ("dp", "row", "col"), scatter_dimension=0, tiled=True),
        lax.psum_scatter(gain_attn_grad, ("dp", "row", "col"), scatter_dimension=0, tiled=True),
        lax.psum_scatter(gain_ffn_grad, ("dp", "row", "col"), scatter_dimension=0, tiled=True),
    )
    ffn_sums = (
        lax.psum(grad_both[:, :ffn_width].astype(jnp.bfloat16), "dp").astype(jnp.float32),
        lax.psum(grad_both[:, ffn_width:].astype(jnp.bfloat16), "dp").astype(jnp.float32),
        lax.psum(grad_down.astype(jnp.bfloat16), "dp").astype(jnp.float32),
    )
    return (
        result,
        tokens_grad,
        grad_sums[0],
        grad_sums[1],
        grad_sums[2],
        grad_sums[3],
        grad_sums[4],
        ffn_sums[0],
        ffn_sums[1],
        ffn_sums[2],
    )


def solution(mesh):
    in_specs = (
        P(("dp", "row", "col"), None),
        P(("dp", "row", "col"), None),
        P(("dp", "row", "col"), None),
        P(("dp", "row", "col"), None),
        P(("dp", "row", "col"), None),
        P(("dp", "row", "col")),
        P(("dp", "row", "col")),
        P("col", "row"),
        P("col", "row"),
        P("row", "col"),
        P("dp", None),
        P("dp", None),
    )
    out_specs = (
        P(("dp", "row"), "col"),
        P(("dp", "row", "col"), None),
        P(("dp", "row", "col"), None),
        P(("dp", "row", "col"), None),
        P(("dp", "row", "col"), None),
        P(("dp", "row", "col")),
        P(("dp", "row", "col")),
        P("col", "row"),
        P("col", "row"),
        P("row", "col"),
    )
    return jax.shard_map(shards, mesh=mesh, in_specs=in_specs, out_specs=out_specs, check_vma=False)
```

profile of v0, /device:TPU:4, one launch (start us, length us, event | category | flops | bytes accessed | tf_op | source)
XLA Modules:
  0.0 2382.4 jit_solution(3695846629108891938)
XLA Ops:
  12.2 41.5 %all-reduce.14 = (bf16[2048]{0:T(1024)(128)(2,1)S(1)}, bf16[2048]{0:T(1024)(128)(2,1)S(1)}) all-reduce(bf16[2048]{0:T(1024)(128)(2,1)S(1)} %dynamic-update-slice, bf16[2048]{0:T(1024)(128)(2,1)S(1)} %dynamic-update-slice.1), channel_id=1, replica_groups=mesh['dp'=4,'row'=4,'col'=2] {'dp','row','col'}, use_global_device_ids=true, to_apply=%add.6 | all-reduce | flops 4096 | bytes 16384
  56.2 9.8 all-gather.13.cloned.1.call-done
  69.7 53.5 %while.34 = (s32[]{:T(128)}, bf16[128,256]{1,0:T(8,128)(2,1)S(1)}, bf16[7,128,256]{2,1,0:T(8,128)(2,1)}, s32[]{:T(128)}) while((s32[]{:T(128)}, bf16[128,256]{1,0:T(8,128)(2,1)S(1)}, bf16[7,128,256]{2,1,0:T(8,128)(2,1)}, s32[]{:T(128)}) %tuple.84), condition=%wide.region_6.7_spmd, body=%wide.region_5.6_spmd.sunk | while | flops 2 | bytes 524393 | solution.py:158
  89.0 5.3 collective-permute-start
  97.5 5.6 collective-permute-start
  105.6 6.2 collective-permute-start
  114.3 5.3 collective-permute-start
  126.9 22.5 all-gather.15.cloned.1.call-done
  149.5 4.9 convolution_bitcast_fusion
  156.8 8.0 fusion.117
  164.8 5.0 fusion.40
  169.9 58.7 %all-gather.17.cloned.1.call-done = bf16[2048,2048]{1,0:T(8,128)(2,1)} async-done(((bf16[64,2048]{1,0:T(8,128)(2,1)}), bf16[2048,2048]{1,0:T(8,128)(2,1)}) %all-gather.17.cloned.1.call-update) | async-done | bytes 8388624 | tf_op jit(solution)/shard_map/all_gather | solution.py:128
  228.5 5.0 multiply_reduce_fusion.3
  234.4 11.8 all_to_all.96
  246.5 44.4 %all-gather.19.cloned.1.call-done = bf16[1024,1024]{1,0:T(8,128)(2,1)} async-done(((bf16[256,1024]{1,0:T(8,128)(2,1)}), bf16[1024,1024]{1,0:T(8,128)(2,1)}) %all-gather.19.cloned.1.call-update) | async-done | bytes 2097168 | tf_op jit(solution)/shard_map/all_gather | solution.py:185
  290.9 12.7 fusion.9
  303.6 143.3 %reduce-scatter.9.cloned.1.call-done = f32[512,3072]{1,0:T(8,128)} async-done(((f32[1024,3072]{1,0:T(8,128)}), f32[512,3072]{1,0:T(8,128)}) %reduce-scatter.9.cloned.1.call-update) | async-done | bytes 6291472 | tf_op jit(solution)/shard_map/reduce_scatter | solution.py:95
  446.9 5.1 fusion.36
  452.0 45.1 %all-gather.21.cloned.1.call-done = bf16[1024,1536]{1,0:T(8,128)(2,1)} async-done(((bf16[512,1536]{1,0:T(8,128)(2,1)}), bf16[1024,1536]{1,0:T(8,128)(2,1)}) %all-gather.21.cloned.1.call-update) | async-done | bytes 3145744 | tf_op jit(solution)/shard_map/all_gather | solution.py:91
  497.1 6.8 fusion.121
  514.4 6.4 all-to-all-done
  520.8 10.8 all_to_all.97
  533.9 47.0 %reduce-scatter.11.cloned.1.call-done = f32[256,1024]{1,0:T(8,128)} async-done(((f32[1024,1024]{1,0:T(8,128)}), f32[256,1024]{1,0:T(8,128)}) %reduce-scatter.11.cloned.1.call-update) | async-done | bytes 1048592 | tf_op jit(solution)/shard_map/reduce_scatter | solution.py:104
  593.8 42.3 %all-reduce.13 = (bf16[2048]{0:T(1024)(128)(2,1)S(1)}, bf16[2048]{0:T(1024)(128)(2,1)S(1)}) all-reduce(bf16[2048]{0:T(1024)(128)(2,1)S(1)} %dynamic-update-slice.2, bf16[2048]{0:T(1024)(128)(2,1)S(1)} %dynamic-update-slice.3), channel_id=1, replica_groups=mesh['dp'=4,'row'=4,'col'=2] {'dp','row','col'}, use_global_device_ids=true, to_apply=%add.8 | all-reduce | flops 4096 | bytes 16384
  643.0 60.3 %while.35 = (s32[]{:T(128)}, bf16[128,256]{1,0:T(8,128)(2,1)}, bf16[7,128,256]{2,1,0:T(8,128)(2,1)}, s32[]{:T(128)}) while((s32[]{:T(128)}, bf16[128,256]{1,0:T(8,128)(2,1)}, bf16[7,128,256]{2,1,0:T(8,128)(2,1)}, s32[]{:T(128)}) %tuple.87), condition=%wide.region_20.21_spmd, body=%wide.region_19.20_spmd.sunk | while | flops 2 | bytes 524393 | solution.py:158
  656.6 5.0 collective-permute-start.1
  665.1 5.2 collective-permute-start.1
  675.0 5.1 collective-permute-start.1
  683.5 5.2 collective-permute-start.1
  692.8 5.8 collective-permute-start.1
  707.1 15.2 all-gather.27.cloned.1.call-done
  722.2 7.1 fusion.109
  737.3 64.7 %all-gather.29.cloned.1.call-done = bf16[2048,2048]{1,0:T(8,128)(2,1)} async-done(((bf16[64,2048]{1,0:T(8,128)(2,1)}), bf16[2048,2048]{1,0:T(8,128)(2,1)}) %all-gather.29.cloned.1.call-update) | async-done | bytes 8388624 | tf_op jit(solution)/shard_map/all_gather | solution.py:128
  801.9 4.9 multiply_reduce_fusion.2
  808.1 11.8 all_to_all.98
  820.0 28.8 %all-gather.23.cloned.1.call-done = bf16[1024,1024]{1,0:T(8,128)(2,1)} async-done(((bf16[256,1024]{1,0:T(8,128)(2,1)}), bf16[1024,1024]{1,0:T(8,128)(2,1)}) %all-gather.23.cloned.1.call-update) | async-done | bytes 2097168 | tf_op jit(solution)/shard_map/all_gather | solution.py:186
  848.7 6.9 fusion.122
  862.7 32.2 %all-gather.31.cloned.1.call-done = bf16[1024,1024]{1,0:T(8,128)(2,1)} async-done(((bf16[256,1024]{1,0:T(8,128)(2,1)}), bf16[1024,1024]{1,0:T(8,128)(2,1)}) %all-gather.31.cloned.1.call-update) | async-done | bytes 2097168 | tf_op jit(solution)/shard_map/all_gather | solution.py:185
  894.9 12.1 fusion.123
  907.1 66.6 %reduce-scatter.13.cloned.1.call-done = f32[512,1536]{1,0:T(8,128)} async-done(((f32[1024,1536]{1,0:T(8,128)}), f32[512,1536]{1,0:T(8,128)}) %reduce-scatter.13.cloned.1.call-update) | async-done | bytes 3145744 | tf_op jit(solution)/shard_map/reduce_scatter | solution.py:95
  973.7 146.7 %reduce-scatter.15.cloned.1.call-done = f32[512,3072]{1,0:T(8,128)} async-done(((f32[1024,3072]{1,0:T(8,128)}), f32[512,3072]{1,0:T(8,128)}) %reduce-scatter.15.cloned.1.call-update) | async-done | bytes 6291472 | tf_op jit(solution)/shard_map/reduce_scatter | solution.py:95
  1120.4 6.0 fusion.27
  1129.1 79.9 %all-gather.33.cloned.1.call-done = bf16[1024,3072]{1,0:T(8,128)(2,1)} async-done(((bf16[512,3072]{1,0:T(8,128)(2,1)}), bf16[1024,3072]{1,0:T(8,128)(2,1)}) %all-gather.33.cloned.1.call-update) | async-done | bytes 6291472 | tf_op jit(solution)/shard_map/all_gather | solution.py:91
  1209.0 12.0 fusion.124
  1221.0 34.4 %all-gather.35.cloned.1.call-done = bf16[1024,1536]{1,0:T(8,128)(2,1)} async-done(((bf16[512,1536]{1,0:T(8,128)(2,1)}), bf16[1024,1536]{1,0:T(8,128)(2,1)}) %all-gather.35.cloned.1.call-update) | async-done | bytes 3145744 | tf_op jit(solution)/shard_map/all_gather | solution.py:91
  1255.4 6.9 convolution_convert_fusion.1
  1262.3 12.1 convolution_convert_fusion
  1274.4 60.5 %reduce-scatter.17.cloned.1.call-done = f32[256,1024]{1,0:T(8,128)} async-done(((f32[1024,1024]{1,0:T(8,128)}), f32[256,1024]{1,0:T(8,128)}) %reduce-scatter.17.cloned.1.call-update) | async-done | bytes 1048592 | tf_op jit(solution)/shard_map/reduce_scatter | solution.py:104
  1340.6 6.0 fusion.113
  1349.8 6.7 convolution_convert_fusion.2
  1371.7 54.3 %while.36 = (s32[]{:T(128)}, f32[128,256]{1,0:T(8,128)S(1)}, f32[7,128,256]{2,1,0:T(8,128)}, s32[]{:T(128)}) while((s32[]{:T(128)}, f32[128,256]{1,0:T(8,128)S(1)}, f32[7,128,256]{2,1,0:T(8,128)}, s32[]{:T(128)}) %tuple.136), condition=%wide.region_30.31_spmd, body=%wide.region_29.30_spmd.sunk | while | flops 98306 | bytes 786537 | solution.py:383
  1387.4 5.2 collective-permute-done.2
  1394.9 5.7 collective-permute-done.2
  1402.9 5.8 collective-permute-done.2
  1410.9 6.4 collective-permute-done.2
  1419.6 5.5 collective-permute-done.2
  1428.3 8.1 fusion.62
  1440.2 8.2 fusion.107
  1448.4 68.8 %all-reduce.18.cloned.1.call-done = (bf16[1024,1536]{1,0:T(8,128)(2,1)}, bf16[1024,1536]{1,0:T(8,128)(2,1)}, bf16[1536,1024]{1,0:T(8,128)(2,1)}) async-done(((bf16[1024,1536]{1,0:T(8,128)(2,1)}, bf16[1024,1536]{1,0:T(8,128)(2,1)}, bf16[1536,1024]{1,0:T(8,128)(2,1)}), (bf16[1024,1536]{1,0:T(8,128)(2,1)}, bf16[1024,1536]{1,0:T(8,128)(2,1)}, bf16[1536,1024]{1,0:T(8,128)(2,1)})) %all-reduce.18.cloned.1.call-update) | async-done | bytes 9437200 | tf_op jit(solution)/shard_map/psum | solution.py:411
  1517.2 5.6 convert_element_type.230
  1536.4 41.6 %all-reduce.12 = (f32[2048]{0:T(1024)S(1)}, f32[2048]{0:T(1024)S(1)}) all-reduce(f32[2048]{0:T(1024)S(1)} %get-tuple-element.109, f32[2048]{0:T(1024)S(1)} %get-tuple-element.107), channel_id=10, replica_groups=mesh['dp'=4,'row'=4,'col'=2] {'dp','row','col'}, use_global_device_ids=true, to_apply=%region_36.37.clone | all-reduce | flops 4096 | bytes 32768
  1582.1 76.2 %reduce-scatter.21.cloned.1.call-done = f32[64,256]{1,0:T(8,128)} async-done(((f32[2048,256]{1,0:T(8,128)}), f32[64,256]{1,0:T(8,128)}) %reduce-scatter.21.cloned.1.call-update) | async-done | bytes 65552 | tf_op jit(solution)/shard_map/reduce_scatter | solution.py:405
  1658.3 356.6 %reduce-scatter.23.cloned.1.call-done = f32[64,2048]{1,0:T(8,128)} async-done(((f32[2048,2048]{1,0:T(8,128)}), f32[64,2048]{1,0:T(8,128)}) %reduce-scatter.23.cloned.1.call-update) | async-done | bytes 524304 | tf_op jit(solution)/shard_map/reduce_scatter | solution.py:406
  2014.9 360.2 %reduce-scatter.19.cloned.1.call-done = f32[64,2048]{1,0:T(8,128)} async-done(((f32[2048,2048]{1,0:T(8,128)}), f32[64,2048]{1,0:T(8,128)}) %reduce-scatter.19.cloned.1.call-update) | async-done | bytes 524304 | tf_op jit(solution)/shard_map/reduce_scatter | solution.py:404
  (328 shorter events, 211.4 us)
Async XLA Ops:
  7.2 489.9 %copy-start = (bf16[1536,1024]{1,0:T(8,128)(2,1)S(1)}, bf16[1536,1024]{1,0:T(8,128)(2,1)}, u32[]{:S(2)}) copy-start(bf16[1536,1024]{1,0:T(8,128)(2,1)} %param.27) | copy-start | bytes 9437188
  7.2 58.9 %all-gather.13.cloned.1.call-start = ((), (), s32[]{:S(2)}) async-start(), calls=%async_computation.14 | async-start | bytes 1081344 | tf_op jit(solution)/shard_map/all_gather | solution.py:127
  7.9 141.5 %all-gather.15.cloned.1.call-start = ((), (), s32[]{:S(2)}) async-start(), calls=%async_computation.15 | async-start | bytes 8650752 | tf_op jit(solution)/shard_map/all_gather | solution.py:126
  8.7 219.8 %all-gather.17.cloned.1.call-start = ((), (), s32[]{:S(2)}) async-start(), calls=%async_computation.16 | async-start | bytes 8650752 | tf_op jit(solution)/shard_map/all_gather | solution.py:128
  9.4 281.5 %all-gather.19.cloned.1.call-start = ((), (), s32[]{:S(2)}) async-start(), calls=%async_computation.17 | async-start | bytes 2621440 | tf_op jit(solution)/shard_map/all_gather | solution.py:185
  69.7 4.5 collective-permute-start
  74.8 6.2 collective-permute-start
  81.6 6.7 collective-permute-start
  89.0 7.9 collective-permute-start
  97.5 7.4 collective-permute-start
  105.6 8.1 collective-permute-start
  114.3 8.3 collective-permute-start
  246.2 200.7 %reduce-scatter.9.cloned.1.call-start = ((), (), s32[]{:S(2)}) async-start(), calls=%async_computation.18 | async-start | bytes 18874368 | tf_op jit(solution)/shard_map/reduce_scatter | solution.py:95
  303.6 193.5 %all-gather.21.cloned.1.call-start = ((), (), s32[]{:S(2)}) async-start(), calls=%async_computation.19 | async-start | bytes 4718592 | tf_op jit(solution)/shard_map/all_gather | solution.py:91
  452.0 128.9 %reduce-scatter.11.cloned.1.call-start = ((), (), s32[]{:S(2)}) async-start(), calls=%async_computation.20 | async-start | bytes 5242880 | tf_op jit(solution)/shard_map/reduce_scatter | solution.py:104
  508.0 76.7 %copy-start.37 = (s32[1,4]{1,0:T(1,128)S(1)}, s32[1,4]{1,0:T(1,128)}, u32[]{:S(2)}) copy-start(s32[1,4]{1,0:T(1,128)} %param.28) | copy-start | bytes 52
  508.0 76.7 %copy-start.38 = (s32[1,4]{1,0:T(1,128)S(1)}, s32[1,4]{1,0:T(1,128)}, u32[]{:S(2)}) copy-start(s32[1,4]{1,0:T(1,128)} %param.29) | copy-start | bytes 52
  508.0 12.8 all-to-all-start
  512.4 126.6 %all-gather.25.cloned.1.call-start = ((), (), s32[]{:S(2)}) async-start(), calls=%async_computation.23 | async-start | bytes 1081344 | tf_op jit(solution)/shard_map/all_gather | solution.py:127
  531.6 61.7 %copy-start.39 = (bf16[64]{0:T(256)(128)(2,1)S(1)}, bf16[64]{0:T(256)(128)(2,1)}, u32[]{:S(2)}) copy-start(bf16[64]{0:T(256)(128)(2,1)} %param.24) | copy-start | bytes 388
  531.6 61.9 %copy-start.40 = (bf16[64]{0:T(256)(128)(2,1)S(1)}, bf16[64]{0:T(256)(128)(2,1)}, u32[]{:S(2)}) copy-start(bf16[64]{0:T(256)(128)(2,1)} %param.23) | copy-start | bytes 388
  583.3 138.9 %all-gather.27.cloned.1.call-start = ((), (), s32[]{:S(2)}) async-start(), calls=%async_computation.24 | async-start | bytes 8650752 | tf_op jit(solution)/shard_map/all_gather | solution.py:126
  584.1 217.9 %all-gather.29.cloned.1.call-start = ((), (), s32[]{:S(2)}) async-start(), calls=%async_computation.25 | async-start | bytes 8650752 | tf_op jit(solution)/shard_map/all_gather | solution.py:128
  587.1 49.4 %all-to-all-start.3 = ((bf16[128,2,1024]{0,2,1:T(8,128)(2,1)}), bf16[128,2,1024]{0,2,1:T(8,128)(2,1)}, u32[]{:S(2)}, u32[]{:S(2)}) async-start(bf16[128,2,1024]{0,2,1:T(8,128)(2,1)} %bitcast.200), calls=%async_computation.5 | async-start | bytes 1048576 | tf_op jit(solution)/shard_map/all_to_all | solution.py:182
  591.3 257.4 %all-gather.23.cloned.1.call-start = ((), (), s32[]{:S(2)}) async-start(), calls=%async_computation.21 | async-start | bytes 2621440 | tf_op jit(solution)/shard_map/all_gather | solution.py:186
  638.5 256.4 %all-gather.31.cloned.1.call-start = ((), (), s32[]{:S(2)}) async-start(), calls=%async_computation.26 | async-start | bytes 2621440 | tf_op jit(solution)/shard_map/all_gather | solution.py:185
  641.2 88.1 %copy-start.28 = (f32[128,64]{0,1:T(8,128)}, f32[128,64]{0,1:T(8,128)S(1)}, u32[]{:S(2)}) copy-start(f32[128,64]{0,1:T(8,128)S(1)} %get-tuple-element.161) | copy-start | bytes 98308
  641.3 88.1 %copy-start.30 = (f32[128,64]{0,1:T(8,128)}, f32[128,64]{0,1:T(8,128)S(1)}, u32[]{:S(2)}) copy-start(f32[128,64]{0,1:T(8,128)S(1)} %get-tuple-element.162) | copy-start | bytes 98308
  643.0 4.7 collective-permute-start.1
  649.0 6.4 collective-permute-start.1
  656.6 7.2 collective-permute-start.1
  665.1 8.6 collective-permute-start.1
  675.0 7.3 collective-permute-start.1
  683.5 8.1 collective-permute-start.1
  692.8 9.2 collective-permute-start.1
  722.2 7.3 copy-start.14
  819.9 153.8 %reduce-scatter.13.cloned.1.call-start = ((), (), s32[]{:S(2)}) async-start(), calls=%async_computation.22 | async-start | bytes 9437184 | tf_op jit(solution)/shard_map/reduce_scatter | solution.py:95
  855.7 264.7 %reduce-scatter.15.cloned.1.call-start = ((), (), s32[]{:S(2)}) async-start(), calls=%async_computation.27 | async-start | bytes 18874368 | tf_op jit(solution)/shard_map/reduce_scatter | solution.py:95
  907.1 302.0 %all-gather.33.cloned.1.call-start = ((), (), s32[]{:S(2)}) async-start(), calls=%async_computation.28 | async-start | bytes 9437184 | tf_op jit(solution)/shard_map/all_gather | solution.py:91
  1128.5 126.9 %all-gather.35.cloned.1.call-start = ((), (), s32[]{:S(2)}) async-start(), calls=%async_computation.33 | async-start | bytes 4718592 | tf_op jit(solution)/shard_map/all_gather | solution.py:91
  1129.1 205.8 %reduce-scatter.17.cloned.1.call-start = ((), (), s32[]{:S(2)}) async-start(), calls=%async_computation.29 | async-start | bytes 5242880 | tf_op jit(solution)/shard_map/reduce_scatter | solution.py:104
  1221.0 34.4 %copy-start.35 = (bf16[1024,1024]{1,0:T(8,128)(2,1)S(1)}, bf16[1024,1024]{1,0:T(8,128)(2,1)}, u32[]{:S(2)}) copy-start(bf16[1024,1024]{1,0:T(8,128)(2,1)} %all-gather.23.cloned.1.call-done) | copy-start | bytes 6291460
  1255.4 6.9 copy-start.36
  1337.0 11.8 all-to-all-start.5
  1340.5 176.7 %all-reduce.18.cloned.1.call-start = ((), (), s32[]{:S(2)}) async-start(), calls=%async_computation.34 | async-start | bytes 18874368 | tf_op jit(solution)/shard_map/psum | solution.py:411
  1346.6 311.7 %reduce-scatter.21.cloned.1.call-start = ((), (), s32[]{:S(2)}) async-start(), calls=%async_computation.31 | async-start | bytes 2162688 | tf_op jit(solution)/shard_map/reduce_scatter | solution.py:405
  1349.7 78.6 %copy-start.6 = (f32[128,2048]{1,0:T(8,128)}, f32[128,2048]{1,0:T(8,128)S(1)}, u32[]{:S(2)}) copy-start(f32[128,2048]{1,0:T(8,128)S(1)} %fusion.52) | copy-start | bytes 3145732
  1349.7 7.0 copy-start.15
  1356.8 6.1 slice-start.1
  1369.4 57.0 %copy-start.4 = (bf16[128,2048]{1,0:T(8,128)(2,1)S(1)}, bf16[128,2048]{1,0:T(8,128)(2,1)}, u32[]{:S(2)}) copy-start(bf16[128,2048]{1,0:T(8,128)(2,1)} %param.18) | copy-start | bytes 1572868
  1371.7 56.6 %copy-start.13 = (bf16[128,16,128]{2,0,1:T(8,128)(2,1)S(1)}, bf16[128,16,128]{2,0,1:T(8,128)(2,1)}, u32[]{:S(2)}) copy-start(bf16[128,16,128]{2,0,1:T(8,128)(2,1)} %fusion.41) | copy-start | bytes 1572868
  1371.7 6.3 collective-permute-start.2
  1379.0 6.2 collective-permute-start.2
  1386.1 6.5 collective-permute-start.2
  1393.6 7.0 collective-permute-start.2
  1401.6 7.1 collective-permute-start.2
  1409.6 7.7 collective-permute-start.2
  1418.3 6.8 collective-permute-start.2
  1428.3 586.6 %reduce-scatter.23.cloned.1.call-start = ((), (), s32[]{:S(2)}) async-start(), calls=%async_computation.32 | async-start | bytes 17301504 | tf_op jit(solution)/shard_map/reduce_scatter | solution.py:406
  1436.5 938.6 %reduce-scatter.19.cloned.1.call-start = ((), (), s32[]{:S(2)}) async-start(), calls=%async_computation.30 | async-start | bytes 17301504 | tf_op jit(solution)/shard_map/reduce_scatter | solution.py:404
  1440.1 8.2 copy-start.10
  1522.9 8.0 slice-start.2
  1532.0 47.2 %copy-start.34 = (f32[128]{0:T(128)S(1)}, f32[128]{0:T(128)}, u32[]{:S(2)}) copy-start(f32[128]{0:T(128)} %copy-done.33) | copy-start | bytes 1540
  1532.0 843.1 %copy-start.1 = (bf16[1536,1024]{1,0:T(8,128)(2,1)S(1)}, bf16[1536,1024]{1,0:T(8,128)(2,1)}, u32[]{:S(2)}) copy-start(bf16[1536,1024]{1,0:T(8,128)(2,1)} %param.27) | copy-start | bytes 9437188
  (26 other events, 73.5 us)
Sparse Core Ops, SparseCore 0:
  11.0 55.0 all-gather.12
  69.1 80.3 all-gather.14
  152.4 76.0 all-gather.16
  246.3 44.5 all-gather.18
  303.7 143.1 reduce-scatter.8
  452.1 44.9 all-gather.20
  504.0 76.7 reduce-scatter.10
  584.3 54.5 all-gather.24
  642.3 79.8 all-gather.26
  725.5 76.4 all-gather.28
  804.2 44.5 all-gather.22
  850.2 44.6 all-gather.30
  897.9 75.7 reduce-scatter.12
  975.9 144.4 reduce-scatter.14
  1128.6 80.3 all-gather.32
  1210.4 44.9 all-gather.34
  1258.1 76.7 reduce-scatter.16
  1346.7 170.5 all-reduce.17
  1520.2 138.0 reduce-scatter.20
  1661.0 353.8 reduce-scatter.22
  2017.7 357.2 reduce-scatter.18
where the time goes:
time: 2400 us; the launch traced here: 2380 us
  waiting for transfers between devices  1850 us (77%)
  blocking collectives  160 us (7%)
  matrix products  153 us (6%)
  starting transfers between devices  90.2 us (4%)
  other arithmetic  62.5 us (3%)
  local copies, waits for them, and re-layouts  55 us (2%)
    reduce_scatter x1, waiting for transfers between devices, shards(): lax.psum_scatter(grad_query, ('dp', 'row', 'col'), scatter_dimension=0, t...  360 us
    reduce_scatter x1, waiting for transfers between devices, shards(): lax.psum_scatter(grad_out, ('dp', 'row', 'col'), scatter_dimension=0, til...  357 us
    reduce_scatter x3, waiting for transfers between devices, column_sum(): lax.psum_scatter(term_fn(jnp.int32(0), row_count * lax.axis_size('col')),...  357 us
    all_gather x3, waiting for transfers between devices, column_gather(): return lax.all_gather(values, 'col', axis=0, tiled=True)  159 us
    unnamed x3, blocking collectives  125 us
    all_gather x2, waiting for transfers between devices, forward_pass(): lax.all_gather(w_out, ('dp', 'row', 'col'), axis=0, tiled=True)  123 us
    reduce_scatter x2, waiting for transfers between devices, row_sum(): lax.psum_scatter(term_fn(jnp.int32(0), row_count * lax.axis_size('row')),...  108 us
    all_gather x2, waiting for transfers between devices, forward_pass(): lax.all_gather(ffn_rows, 'row', axis=0, tiled=True)  76.7 us
  transfers between devices with their start and end apart: 45, of which 43 were waited for; matrix products, arithmetic and copies ran while one was open for 9% of the time, Pallas kernels for 0%

commit v1 on v0

v1 whole, which is shorter than its diff:
```python
import functools
import math

import jax
import jax.numpy as jnp
from jax import lax
from jax.experimental import pallas as pl
from jax.experimental.pallas import tpu as pltpu
from jax.sharding import PartitionSpec as P

HEADS = 16
HEAD = 128

EPSILON = 1e-06
ROPE_BASE = 10000.0
NEG_FILL = -1e30
SCALE = 1.0 / math.sqrt(HEAD)
DP = ("y", "core")
EVERY = ("y", "core", "row", "col")
F32 = jnp.float32
BF16 = jnp.bfloat16
MIB = 2**20


def swap_core(value):
    return lax.ppermute(value, "core", [(0, 1), (1, 0)])


def swap_y(value, k):
    return lax.ppermute(value, "y", [(i, i ^ k) for i in range(lax.axis_size("y"))])


def swap_col(value):
    return lax.ppermute(value, "col", [(0, 1), (1, 0)])


def deal(value, axes):
    return lax.all_to_all(value, axes, split_axis=0, concat_axis=0, tiled=True)


def transpose_devices(value):
    n_dp, n_row, n_col = 2 * lax.axis_size("y"), lax.axis_size("row"), lax.axis_size("col")
    pairs = [
        ((d * n_row + r) * n_col + c, (r * n_row + d) * n_col + c)
        for d in range(n_dp)
        for r in range(n_row)
        for c in range(n_col)
    ]
    return lax.ppermute(value, EVERY, pairs)


def after(value, *others):
    return lax.optimization_barrier((value,) + others)[0]


def dot(left, right):
    return jnp.dot(left, right, preferred_element_type=F32)


def dot_tn(left, right):
    return lax.dot_general(left, right, (((0,), (0,)), ((), ())), preferred_element_type=F32)


def dot_nt(left, right):
    return lax.dot_general(left, right, (((1,), (1,)), ((), ())), preferred_element_type=F32)


def inv_rms(values):
    return lax.rsqrt(jnp.mean(values * values, axis=-1, keepdims=True) + EPSILON)


def run(body, ids, args, in_specs, outs, out_specs, grid=(1,), scratch=(), limit=56):
    def place(spec, array):
        if spec is None:
            zeros = (0,) * len(array.shape)
            return pl.BlockSpec(array.shape, lambda *_: zeros)
        return spec

    in_specs = [place(s, a) for s, a in zip(in_specs, args)]
    out_specs = [place(s, a) for s, a in zip(out_specs, outs)]
    return pl.pallas_call(
        body,
        grid_spec=pltpu.PrefetchScalarGridSpec(
            num_scalar_prefetch=1,
            grid=grid,
            in_specs=in_specs,
            out_specs=out_specs,
            scratch_shapes=list(scratch),
        ),
        out_shape=outs,
        compiler_params=pltpu.CompilerParams(
            vmem_limit_bytes=limit * MIB, dimension_semantics=("arbitrary",) * len(grid)
        ),
        cost_estimate=pl.CostEstimate(flops=0, bytes_accessed=10**5, transcendentals=0),
    )(ids, *args)


def sds(shape, dtype=BF16):
    return jax.ShapeDtypeStruct(shape, dtype)


def turn(values, cos_part, sin_part):
    return values * cos_part + pltpu.roll(values, HEAD // 2, 1) * sin_part


def cut_body(ids, g_ref, u_ref, d_ref, g_out, u_out, d_out):
    g_out[...] = g_ref[...]
    u_out[...] = u_ref[...]
    d_out[...] = d_ref[...]


def pack_body(n_row, ids, wq_ref, wkv_ref, ga_ref, gf_ref, out_ref):
    shard, kv = wkv_ref.shape
    hcols = wq_ref.shape[1] // n_row
    used = hcols + kv
    for r in range(n_row):
        out_ref[r, :shard, :hcols] = wq_ref[:, r * hcols : (r + 1) * hcols]
        out_ref[r, :shard, hcols:] = wkv_ref[...]
        line = lax.broadcasted_iota(jnp.int32, (16, used), 0)
        ga = jnp.broadcast_to(ga_ref[...].astype(F32), (16, used))
        gf = jnp.broadcast_to(gf_ref[...].astype(F32), (16, used))
        tail = jnp.where(line == 0, ga, jnp.where(line == 1, gf, 0.0))
        out_ref[r, shard:, :] = tail.astype(BF16)


def front_body(n_row, n_col, hcols, shard, ids, x_ref, own_ref, oth_ref, cos_ref, sin_ref, *refs):
    a_ref, kv_ref, q_ref, w_ref, gain_ref, g0, g1 = refs
    core = ids[0] & 1
    tall = shard + 16
    width = a_ref.shape[1]
    for flip, pack in ((0, own_ref), (1, oth_ref)):
        for p in range(pack.shape[0]):
            y, c = p // n_col, p % n_col
            for z in range(n_row):
                place = ((y * 2 + (core ^ flip)) * n_row + z) * n_col + c
                rows = pl.ds(pl.multiple_of(place * shard, shard), shard)
                w_ref[rows, :] = pack[p, z * tall : z * tall + shard, :]
                tail = pack[p, z * tall + shard : (z + 1) * tall, :HEAD].astype(F32)
                g0[pl.ds(place, 1), :] = tail[0:1]
                g1[pl.ds(place, 1), :] = tail[1:2]
    count = width // shard
    pick = lax.broadcasted_iota(jnp.int32, (HEAD, width), 0)
    feature = lax.broadcasted_iota(jnp.int32, (HEAD, width), 1)
    spread = ((feature & (shard - 1)) == pick).astype(F32)
    home = lax.broadcasted_iota(jnp.int32, (count, width), 0)
    mine = (lax.broadcasted_iota(jnp.int32, (count, width), 1) & ~(shard - 1)) == home * shard
    lines = []
    for g in (g0, g1):
        wide = jnp.dot(g[...], spread, preferred_element_type=F32)
        lines.append(jnp.sum(jnp.where(mine, wide, 0.0), axis=0, keepdims=True))
    gain = lines[0]
    gain_ref[...] = jnp.concatenate(lines * 4, axis=0)
    rows_all = x_ref.shape[0]
    step = 128
    for r in range(rows_all // step):
        rows = slice(r * step, (r + 1) * step)
        x = x_ref[rows, :].astype(F32)
        a_ref[rows, :] = (x * inv_rms(x) * gain).astype(BF16)
    kv = dot(a_ref[...], w_ref[:, hcols:])
    key = turn(kv[:, :HEAD], cos_ref[...], sin_ref[...])
    kv_ref[:, :HEAD] = key.astype(BF16)
    kv_ref[:, HEAD:] = kv[:, HEAD:].astype(BF16)
    raw = dot(a_ref[...], w_ref[:, :hcols])
    for h in range(hcols // HEAD):
        cols = slice(h * HEAD, (h + 1) * HEAD)
        q_ref[:, cols] = (turn(raw[:, cols], cos_ref[...], sin_ref[...]) * SCALE).astype(BF16)


def stack_heads(block, heads):
    return jnp.concatenate([block[:, h * HEAD : (h + 1) * HEAD] for h in range(heads)], axis=0)


def key_masks(lo, hi, count, n, n_col, col):
    j = lax.broadcasted_iota(jnp.int32, (1, count), 1)
    at = j + (j - (j & (n - 1))) * (n_col - 1)
    own, oth = at + col * n, at + (1 - col) * n
    return (own >= lo) & (own <= hi), (oth >= lo) & (oth <= hi)


def attend_body(n_row, n_col, heads, ids, q_ref, own_ref, oth_ref, lo_ref, hi_ref, m_ref, l_ref):
    col = ids[2]
    n = q_ref.shape[0] // n_row
    for r in range(n_row):
        rows = slice(r * n, (r + 1) * n)
        count = (r + 1) * n
        q = stack_heads(q_ref[rows, :], heads)
        lo = jnp.concatenate([lo_ref[rows, :]] * heads, axis=0)
        hi = jnp.concatenate([hi_ref[rows, :]] * heads, axis=0)
        ok_own, ok_oth = key_masks(lo, hi, count, n, n_col, col)
        s_own = jnp.where(ok_own, dot_nt(q, own_ref[:count, :HEAD]), NEG_FILL)
        s_oth = jnp.where(ok_oth, dot_nt(q, oth_ref[:count, :HEAD]), NEG_FILL)
        peak = jnp.maximum(
            jnp.max(s_own, axis=-1, keepdims=True), jnp.max(s_oth, axis=-1, keepdims=True)
        )
        e_own = jnp.where(ok_own, jnp.exp(s_own - peak), 0.0)
        e_oth = jnp.where(ok_oth, jnp.exp(s_oth - peak), 0.0)
        total = jnp.sum(e_own, axis=-1, keepdims=True) + jnp.sum(e_oth, axis=-1, keepdims=True)
        share = 1.0 / total
        mixed = dot((e_own * share).astype(BF16), own_ref[:count, HEAD:]) + dot(
            (e_oth * share).astype(BF16), oth_ref[:count, HEAD:]
        )
        for h in range(heads):
            m_ref[rows, h * HEAD : (h + 1) * HEAD] = mixed[h * n : (h + 1) * n].astype(BF16)
        log_total = peak + jnp.log(total)
        for h in range(heads):
            l_ref[rows, h : h + 1] = log_total[h * n : (h + 1) * n]


def branch_body(n_col, ids, mixed_ref, own_ref, oth_ref, part_ref, w_ref):
    core = ids[0] & 1
    shard = own_ref.shape[1]
    for flip, piece in ((0, own_ref), (1, oth_ref)):
        for p in range(piece.shape[0]):
            place = ((p // n_col) * 2 + (core ^ flip)) * n_col + p % n_col
            rows = pl.ds(pl.multiple_of(place * shard, shard), shard)
            w_ref[rows, :] = piece[p]
    part_ref[...] = dot(mixed_ref[...], w_ref[...]).astype(BF16)


def norm_body(ids, x_ref, branch_ref, gain_ref, f_ref):
    resid = x_ref[...].astype(F32) + branch_ref[...].astype(F32)
    f_ref[...] = (resid * inv_rms(resid) * gain_ref[1:2, :]).astype(BF16)


def ffn_spans(dp, col, half, chunk, n_dp):
    return [pl.ds(pl.multiple_of(col * half, half), half)] + [
        pl.ds(pl.multiple_of((1 - col) * half + (dp ^ a) * chunk, chunk), chunk)
        for a in range(n_dp)
    ]


def ffn_body(n_dp, tiles, ids, f_ref, c_ref, *refs):
    count = n_dp + 1
    gates, ups, downs = refs[:count], refs[count : 2 * count], refs[2 * count : 3 * count]
    h_ref, dg_ref, du_ref, out_ref, sd_ref, sg_ref, su_ref = refs[3 * count : 3 * count + 7]
    acc, h_scr, dg_scr, du_scr, into_scr, down_scr = refs[3 * count + 7 :]
    step = pl.program_id(0)
    half, tile = gates[0].shape
    col = ids[2]
    spans = ffn_spans(ids[0], col, half, gates[1].shape[0], n_dp)

    @pl.when(step == 0)
    def _():
        acc[...] = jnp.zeros_like(acc)

    @pl.when(step < tiles)
    def _():
        for span, g, u, d in zip(spans, gates, ups, downs):
            into_scr[span, :tile] = g[...]
            into_scr[span, tile:] = u[...]
            down_scr[:, span] = d[...]
        f = f_ref[...]
        gate, up = dot(f, into_scr[:, :tile]), dot(f, into_scr[:, tile:])
        d_hid = dot_nt(c_ref[...], down_scr[...])
        root = math.sqrt(2.0 / math.pi)
        square = gate * gate
        tanh = jnp.tanh(gate * (root + (root * 0.044715) * square))
        bell = 0.5 + 0.5 * tanh
        slope = bell + (0.5 * gate) * (1.0 - tanh * tanh) * (root + (3 * root * 0.044715) * square)
        act = gate * bell
        hidden = (act * up).astype(BF16)
        d_gate = (d_hid * up * slope).astype(BF16)
        d_up = (d_hid * act).astype(BF16)
        units = pl.ds(pl.multiple_of(step * tile, tile), tile)
        for out, scr, value in (
            (h_ref, h_scr, hidden),
            (dg_ref, dg_scr, d_gate),
            (du_ref, du_scr, d_up),
        ):
            out[...] = value
            scr[:, units] = value
        acc[...] += dot_nt(jnp.concatenate([d_gate, d_up], axis=1), into_scr[...])

    @pl.when(step == tiles - 1)
    def _():
        out_ref[...] = acc[...].astype(BF16)

    @pl.when(step >= tiles)
    def _():
        side = (1 - (step - tiles)) ^ col
        core = (ids[0] & 1) ^ 1
        rows, units = sg_ref.shape[1], sd_ref.shape[1]
        left = f_ref[:, pl.ds(pl.multiple_of((side * 2 + core) * rows, rows), rows)].T
        for out, scr in ((sg_ref, dg_scr), (su_ref, du_scr)):
            for j in range(tiles):
                cols = slice(j * tile, (j + 1) * tile)
                out[0, :, cols] = dot(left, scr[:, cols]).astype(BF16)
        cot = c_ref[:, pl.ds(pl.multiple_of(side * half, half), half)]
        cut = units // 3
        for k in range(3):
            place = pl.multiple_of(core * units + k * cut, cut)
            left = h_scr[:, pl.ds(place, cut)].T
            sd_ref[0, k * cut : (k + 1) * cut, :] = dot(left, cot).astype(BF16)


def down_body(n_dp, ids, h_ref, *refs):
    downs = refs[: n_dp + 1]
    out_ref = refs[n_dp + 1]
    spans = ffn_spans(ids[0], ids[2], downs[0].shape[1], downs[1].shape[1], n_dp)
    for span, d in zip(spans, downs):
        out_ref[:, span] = dot(h_ref[...], d[...]).astype(BF16)


def grad_in_body(tile, ids, f_ref, d_ref, got_ref, theirs_ref, mine_ref):
    rows = mine_ref.shape[0]
    for i, out in enumerate((theirs_ref, mine_ref)):
        place = (((1 - i) ^ ids[2]) * 2 + (ids[0] & 1)) * rows
        left = f_ref[:, pl.ds(pl.multiple_of(place, rows), rows)].T
        for j in range(d_ref.shape[1] // tile):
            cols = slice(j * tile, (j + 1) * tile)
            res = dot(left, d_ref[:, cols]) + got_ref[i, :, cols].astype(F32)
            out[:, cols] = res.astype(BF16)


def grad_in_y_body(tile, ids, f_ref, d_ref, got_ref, *outs):
    rows = outs[0].shape[0]
    y = ids[0] // 2
    for h in range(2):
        for i in range(2):
            cut = ((1 - h) ^ y) * rows
            place = (((1 - i) ^ ids[2]) * 2 + (ids[0] & 1)) * 2 * rows + cut
            left = f_ref[:, pl.ds(pl.multiple_of(place, rows), rows)].T
            got = got_ref.at[i, pl.ds(pl.multiple_of(cut, rows), rows)]
            for j in range(d_ref.shape[1] // tile):
                cols = slice(j * tile, (j + 1) * tile)
                res = dot(left, d_ref[:, cols]) + got[:, cols].astype(F32)
                outs[h * 2 + i][:, cols] = res.astype(BF16)


def grad_down_body(tile, ids, h_ref, c_ref, got_ref, first_ref, second_ref, mine_ref):
    units, half = mine_ref.shape
    cut = half // 2
    for k in range(units // tile):
        place = pl.multiple_of((ids[0] & 1) * units + k * tile, tile)
        left = h_ref[:, pl.ds(place, tile)].T
        rows = slice(k * tile, (k + 1) * tile)
        for i in range(2):
            cols = pl.ds(pl.multiple_of(((1 - i) ^ ids[2]) * half, half), half)
            res = (dot(left, c_ref[:, cols]) + got_ref[i, rows, :].astype(F32)).astype(BF16)
            if i == 0:
                first_ref[rows, :] = res[:, :cut]
                second_ref[rows, :] = res[:, cut:]
            else:
                mine_ref[rows, :] = res


def own_body(ids, d_ref, x_ref, branch_ref, cot_ref, gain_ref, dres_ref, low_ref, part_ref):
    resid = x_ref[...].astype(F32) + branch_ref[...].astype(F32)
    r2 = inv_rms(resid)
    n2 = resid * r2
    d = d_ref[...].astype(F32)
    u = d * gain_ref[1:2, :]
    d_resid = cot_ref[...].astype(F32) + r2 * (u - n2 * jnp.mean(u * n2, axis=-1, keepdims=True))
    dres_ref[...] = d_resid
    low_ref[...] = d_resid.astype(BF16)
    part_ref[...] = jnp.broadcast_to(jnp.sum(d * n2, axis=0, keepdims=True), part_ref.shape)


def attend_back_body(n_row, n_col, heads, ids, *refs):
    q_ref, own_ref, oth_ref, lo_ref, hi_ref, l_ref, cos_ref, sin_ref = refs[:8]
    refs = refs[8:]
    db_ref, w_ref, dq_ref, out_ref, kv_own, kv_oth, dm_ref = refs
    dm_ref[...] = dot_nt(db_ref[...], w_ref[...]).astype(BF16)
    col = ids[2]
    n = q_ref.shape[0] // n_row
    kv_own[...] = jnp.zeros_like(kv_own)
    kv_oth[...] = jnp.zeros_like(kv_oth)
    for r in range(n_row):
        rows = slice(r * n, (r + 1) * n)
        count = (r + 1) * n
        q = stack_heads(q_ref[rows, :], heads)
        dm = stack_heads(dm_ref[rows, :], heads)
        lo = jnp.concatenate([lo_ref[rows, :]] * heads, axis=0)
        hi = jnp.concatenate([hi_ref[rows, :]] * heads, axis=0)
        log_total = jnp.concatenate([l_ref[rows, h : h + 1] for h in range(heads)], axis=0)
        oks = key_masks(lo, hi, count, n, n_col, col)
        probs, d_probs = [], []
        for ok, kv_ref in zip(oks, (own_ref, oth_ref)):
            scores = dot_nt(q, kv_ref[:count, :HEAD])
            probs.append(jnp.where(ok, jnp.exp(jnp.where(ok, scores - log_total, NEG_FILL)), 0.0))
            d_probs.append(dot_nt(dm, kv_ref[:count, HEAD:]))
        mean = jnp.sum(probs[0] * d_probs[0], axis=-1, keepdims=True) + jnp.sum(
            probs[1] * d_probs[1], axis=-1, keepdims=True
        )
        dq = None
        for p, dpr, kv_ref, acc in zip(probs, d_probs, (own_ref, oth_ref), (kv_own, kv_oth)):
            ds = (p * (dpr - mean)).astype(BF16)
            part = dot(ds, kv_ref[:count, :HEAD])
            dq = part if dq is None else dq + part
            acc[:count, :HEAD] += dot_tn(ds, q)
            acc[:count, HEAD:] += dot_tn(p.astype(BF16), dm)
        cos_part, sin_part = cos_ref[rows, :], sin_ref[rows, :]
        for h in range(heads):
            piece = turn(dq[h * n : (h + 1) * n], cos_part, -sin_part) * SCALE
            dq_ref[rows, h * HEAD : (h + 1) * HEAD] = piece.astype(BF16)
    for r in range(n_row):
        rows = slice(r * n, (r + 1) * n)
        out_ref[r * n_col + col] = kv_own[rows, :].astype(BF16)
        out_ref[r * n_col + 1 - col] = kv_oth[rows, :].astype(BF16)


def keyval_body(ids, cos_ref, sin_ref, pieces_ref, out_ref):
    total = jnp.sum(pieces_ref[...].astype(F32), axis=0)
    out_ref[:, :HEAD] = turn(total[:, :HEAD], cos_ref[...], -sin_ref[...]).astype(BF16)
    out_ref[:, HEAD:] = total[:, HEAD:].astype(BF16)


def deal_rows(n_row, n_col, shard, ids, res, line_of, send_ref, keep_ref):
    step = pl.program_id(0)
    other = (step & 1) == 0
    for r in range(n_row):
        for c in range(n_col):
            k = r * n_col + c
            block = res[k * shard : (k + 1) * shard]
            if line_of is not None:
                line = lax.broadcasted_iota(jnp.int32, (16, res.shape[1]), 0)
                wide = jnp.broadcast_to(line_of(k), (16, res.shape[1]))
                pad = jnp.where(line == 0, wide, 0.0).astype(BF16)
                block = jnp.concatenate([block, pad], axis=0)
            tall = block.shape[0]
            spot = (step // 2) * n_col + c

            @pl.when(other)
            def _():
                send_ref[spot, r * tall : (r + 1) * tall, :] = block

            @pl.when(jnp.logical_not(other))
            def _():
                keep_ref[spot, r * tall : (r + 1) * tall, :] = block


def project_out_body(n_dp, n_col, ids, mixed_ref, db_ref, send_ref, keep_ref, scr):
    scr[...] = mixed_ref[...].T
    shard = send_ref.shape[1]
    rows = n_col * shard
    for y in range(n_dp // 2):
        for flip, out in ((1, send_ref), (0, keep_ref)):
            place = pl.multiple_of((y * 2 + ((ids[0] & 1) ^ flip)) * rows, rows)
            res = dot(scr[pl.ds(place, rows), :], db_ref[...]).astype(BF16)
            for c in range(n_col):
                out[y * n_col + c] = res[c * shard : (c + 1) * shard]


def project_in_body(n_row, n_col, shard, ids, left_ref, dq_ref, dkv_ref, gain_ref, *refs):
    send_ref, keep_ref, scr = refs
    scr[...] = left_ref[...].T
    n = dkv_ref.shape[0]
    own = scr[:, pl.ds(pl.multiple_of(ids[1] * n, n), n)]
    res = jnp.concatenate(
        [dot(scr[...], dq_ref[...]).astype(BF16), dot(own, dkv_ref[...]).astype(BF16)], axis=1
    )
    deal_rows(
        n_row, n_col, shard, ids, res, lambda k: gain_ref[k : k + 1, :], send_ref, keep_ref
    )


def attn_grad_body(ids, d_ref, w_ref, out_ref):
    out_ref[...] = dot_nt(d_ref[...], w_ref[:, : d_ref.shape[1]]).astype(BF16)


def token_body(ids, d_ref, dkv_ref, wkv_ref, x_ref, gain_ref, dres_ref, out_ref):
    d = d_ref[...].astype(F32) + dot_nt(dkv_ref[...], wkv_ref[:, wkv_ref.shape[1] - 2 * HEAD :])
    x = x_ref[...].astype(F32)
    r1 = inv_rms(x)
    n1 = x * r1
    u = d * gain_ref[0:1, :]
    out = dres_ref[...] + r1 * (u - n1 * jnp.mean(u * n1, axis=-1, keepdims=True))
    out_ref[...] = out.astype(BF16)


def last_body(n_row, hcols, ids, pieces_ref, wq_ref, wkv_ref, gain_ref, *refs):
    gq_ref, gkv_ref, ga_ref, gf_ref = refs
    shard = gq_ref.shape[0]
    gkv = jnp.sum(pieces_ref[:, :shard, hcols:].astype(F32), axis=0)
    gkv_ref[...] = gkv
    gf_ref[...] = jnp.sum(pieces_ref[:, shard:, :].astype(F32), axis=0)[:8]
    total = jnp.sum(gkv * wkv_ref[...].astype(F32), axis=-1, keepdims=True)
    for r in range(n_row):
        cols = slice(r * hcols, (r + 1) * hcols)
        part = pieces_ref[r, :shard, :hcols].astype(F32)
        gq_ref[:, cols] = part
        total = total + jnp.sum(part * wq_ref[:, cols].astype(F32), axis=-1, keepdims=True)
    ga_ref[...] = total / gain_ref[...]


def join_body(ids, mine_ref, rest_ref, out_ref):
    rows = out_ref.shape[0]
    count = mine_ref.shape[0] // rows
    step = pl.program_id(0)
    place = pl.ds(pl.multiple_of((step % count) * rows, rows), rows)
    mine = (ids[0] & 1) == step // count

    @pl.when(mine)
    def _():
        out_ref[...] = mine_ref[place, :].astype(F32)

    @pl.when(jnp.logical_not(mine))
    def _():
        out_ref[...] = rest_ref[place, :].astype(F32)


def join_four_body(ids, own_ref, other_ref, own_rest_ref, other_rest_ref, out_ref):
    step = pl.program_id(0)
    core, y = ids[0] & 1, ids[0] // 2
    for flip, parts in ((0, (own_ref, other_ref)), (1, (own_rest_ref, other_rest_ref))):
        for k, part in enumerate(parts):

            @pl.when(step == (core ^ flip) * 2 + (y ^ k))
            def _():
                out_ref[...] = part[...].astype(F32)


def layout(length_row, order_row, where_at):
    slot_ids = jnp.arange(length_row.shape[0], dtype=jnp.int32)
    placed = jnp.sum(
        jnp.where(order_row[:, None] == slot_ids[None, :], length_row[None, :], 0),
        axis=1,
        dtype=jnp.int32,
    )
    before = jnp.where(slot_ids[None, :] < slot_ids[:, None], placed[None, :], 0)
    starts = jnp.sum(before, axis=1, dtype=jnp.int32)
    ends = starts + placed
    within = (where_at[:, None] >= starts[None, :]) & (where_at[:, None] < ends[None, :])
    begin = jnp.sum(jnp.where(within, starts[None, :], 0), axis=1, dtype=jnp.int32)
    return jnp.where(where_at < jnp.sum(placed), where_at - begin, 0)


def add_body(ids, left_ref, right_ref, out_ref):
    out_ref[...] = (left_ref[...].astype(F32) + right_ref[...].astype(F32)).astype(BF16)


def three_body(ids, a_ref, b_ref, c_ref, out_ref):
    total = a_ref[...].astype(F32) + b_ref[...].astype(F32) + c_ref[...].astype(F32)
    out_ref[...] = total.astype(BF16)


def beside_body(ids, left_ref, first_ref, second_ref, out_ref):
    cut = first_ref.shape[1]
    for k, part in enumerate((first_ref, second_ref)):
        cols = slice(k * cut, (k + 1) * cut)
        total = left_ref[:, cols].astype(F32) + part[...].astype(F32)
        out_ref[:, cols] = total.astype(BF16)


def tile_of(size, wanted):
    while size % wanted:
        wanted //= 2
    return wanted


def shards(
    tokens,
    cotangent,
    w_query,
    w_keyval,
    w_out,
    norm_attn,
    norm_ffn,
    w_gate,
    w_up,
    w_down,
    lengths,
    placement,
):
    n_y, n_row, n_col = lax.axis_size("y"), lax.axis_size("row"), lax.axis_size("col")
    n_dp = 2 * n_y
    dp, row, col = lax.axis_index(DP), lax.axis_index("row"), lax.axis_index("col")
    ids = jnp.stack([dp, row, col]).astype(jnp.int32)
    n, width = tokens.shape
    half = width // n_col
    rows_all = n_row * n
    heads = HEADS // n_row
    hcols = heads * HEAD
    part = width // n_row
    shard = w_query.shape[0]
    ffn = w_gate.shape[1]
    chunk = half // n_dp
    used = hcols + 2 * HEAD
    tall = shard + 16

    def add_low(left, right):
        return run(add_body, ids, [left, right], [None, None], [sds(left.shape)], [None])[0]

    zeros = jnp.zeros((1, used - shard), BF16)
    pack = run(
        functools.partial(pack_body, n_row),
        ids,
        [w_query, w_keyval]
        + [jnp.concatenate([g[None, :], zeros], axis=1) for g in (norm_attn, norm_ffn)],
        [None] * 4,
        [sds((n_row, tall, used))],
        [None],
    )[0]
    packed = deal(pack, "row").reshape(1, n_row * tall, used)
    x_low = lax.all_gather(tokens, "row", axis=0, tiled=True)
    wo_turned = transpose_devices(after(w_out, packed))[None]
    around = n_y * n_col
    pack_own = deal(jnp.broadcast_to(packed, (around,) + packed.shape[1:]), ("y", "col"))
    pack_oth = swap_core(pack_own)
    cot = lax.all_gather(after(cotangent, pack_own), "row", axis=0, tiled=True)

    where_at = (
        (jnp.arange(n_row, dtype=jnp.int32) * (n_col * n))[:, None]
        + jnp.arange(n, dtype=jnp.int32)
        + col * n
    ).reshape(-1)
    offset = layout(lengths[0], placement[0], where_at)
    low_at, high_at = (where_at - offset)[:, None], where_at[:, None]
    frequency = ROPE_BASE ** (-2.0 * jnp.arange(HEAD // 2, dtype=jnp.int32).astype(F32) / HEAD)
    angle = offset.astype(F32)[:, None] * frequency[None, :]
    cos_part, sin_part = jnp.cos(angle), jnp.sin(angle)
    cos_all = jnp.concatenate([cos_part, cos_part], axis=1)
    sin_all = jnp.concatenate([-sin_part, sin_part], axis=1)

    attn_in, kv_own, query, w_qkv, gains = run(
        functools.partial(front_body, n_row, n_col, hcols, shard),
        ids,
        [x_low, pack_own, pack_oth, cos_all, sin_all],
        [None, None, None, None, None],
        [
            sds((rows_all, width)),
            sds((rows_all, 2 * HEAD)),
            sds((rows_all, hcols)),
            sds((width, used)),
            sds((8, width), F32),
        ],
        [None, None, None, None, None],
        scratch=[pltpu.VMEM((width // shard, HEAD), F32)] * 2,
    )
    kv_oth = swap_col(kv_own)
    wo_own = deal(
        jnp.broadcast_to(after(wo_turned, kv_own), (around,) + wo_turned.shape[1:]),
        ("y", "col"),
    )
    mixed, log_total = run(
        functools.partial(attend_body, n_row, n_col, heads),
        ids,
        [query, kv_own, kv_oth, low_at, high_at],
        [None] * 5,
        [sds((rows_all, hcols)), sds((rows_all, HEAD), F32)],
        [None] * 2,
    )
    wo_oth = swap_core(after(wo_own, mixed))
    gate_cut, up_cut, down_cut = run(
        cut_body,
        ids,
        [w_gate, w_up, after(w_down, mixed)],
        [pl.BlockSpec((chunk, ffn), lambda i, ids: (ids[0], 0))] * 2
        + [pl.BlockSpec((ffn, chunk), lambda i, ids: (0, ids[0]))],
        [sds((chunk, ffn))] * 2 + [sds((ffn, chunk))],
        [None] * 3,
    )
    gate_got = swap_col(gate_cut)
    up_got = swap_col(after(up_cut, gate_got))
    down_got = swap_col(after(down_cut, up_got))
    gate_y = [gate_got] + [swap_y(gate_got, k) for k in range(1, n_y)]
    up_y = [up_got] + [swap_y(up_got, k) for k in range(1, n_y)]
    down_y = [down_got] + [swap_y(down_got, k) for k in range(1, n_y)]
    part_branch, w_rows = run(
        functools.partial(branch_body, n_col),
        ids,
        [mixed, wo_own, wo_oth],
        [None, None, None],
        [sds((rows_all, width)), sds((hcols, width))],
        [None] * 2,
    )
    branch = lax.psum_scatter(after(part_branch, cot), "row", scatter_dimension=0, tiled=True)
    ffn_own_in = run(
        norm_body,
        ids,
        [tokens, after(branch, up_got, *gate_y), gains],
        [None] * 3,
        [sds((n, width))],
        [None],
    )[0]
    ffn_in = lax.all_gather(ffn_own_in, "row", axis=0, tiled=True)

    def with_core(own, around_y):
        return [own] + [x for g in around_y for x in (g, swap_core(after(g, part_branch)))]

    gates, ups, downs = (
        with_core(w_gate, gate_y),
        with_core(w_up, up_y),
        with_core(w_down, down_y),
    )

    tile = tile_of(ffn, 512)
    tiles = ffn // tile
    quarter = half // 2

    def at(j):
        return jnp.minimum(j, tiles - 1)

    def once(array):
        zeros = (0,) * len(array.shape)
        return pl.BlockSpec(array.shape, lambda *_: zeros, pipeline_mode=pl.Buffered(1))

    into = [pl.BlockSpec((half, tile), lambda j, ids: (0, at(j)))] + [
        pl.BlockSpec((chunk, tile), lambda j, ids: (0, at(j)))
    ] * n_dp
    late = lambda j, ids: (jnp.maximum(j - tiles, 0), 0, 0)
    hidden, d_gate, d_up, d_ffn, sent_down, sent_gate, sent_up = run(
        functools.partial(ffn_body, n_dp, tiles),
        ids,
        [ffn_in, cot] + gates + ups + downs,
        [once(ffn_in), once(cot)]
        + into * 2
        + [pl.BlockSpec((tile, half), lambda j, ids: (at(j), 0))]
        + [pl.BlockSpec((tile, chunk), lambda j, ids: (at(j), 0))] * n_dp,
        [sds((rows_all, ffn))] * 3
        + [sds((rows_all, width)), sds((2, ffn // 2, half))]
        + [sds((2, quarter, ffn))] * 2,
        [pl.BlockSpec((rows_all, tile), lambda j, ids: (0, at(j)))] * 3
        + [None, pl.BlockSpec((1, ffn // 2, half), late)]
        + [pl.BlockSpec((1, quarter, ffn), late)] * 2,
        grid=(tiles + 2,),
        scratch=[pltpu.VMEM((rows_all, width), F32)]
        + [pltpu.VMEM((rows_all, ffn), BF16)] * 3
        + [pltpu.VMEM((width, 2 * tile), BF16), pltpu.VMEM((tile, width), BF16)],
        limit=60,
    )
    d_own = lax.psum_scatter(d_ffn, "row", scatter_dimension=0, tiled=True)

    ft = tile_of(ffn, 512)
    rt = tile_of(ffn // 2, 256)

    def grad_in(right, got, *gate_on):
        body = functools.partial(grad_in_body, ft)
        args = [after(ffn_in, *gate_on), right, got]
        return run(body, ids, args, [None] * 3, [sds((quarter, ffn))] * 2, [None] * 2)

    def grad_in_y(right, got, *gate_on):
        return run(
            functools.partial(grad_in_y_body, ft),
            ids,
            [after(ffn_in, *gate_on), right, got],
            [None, None, None],
            [sds((quarter // 2, ffn))] * 4,
            [None] * 4,
        )

    def grad_down_part(got, *gate_on):
        body = functools.partial(grad_down_body, rt)
        args = [after(hidden, *gate_on), cot, got]
        outs = [sds((ffn // 2, half // 2))] * 2 + [sds((ffn // 2, half))]
        return run(body, ids, args, [None] * 3, outs, [None] * 3)

    got_down = swap_core(sent_down)
    got_gate = swap_core(sent_gate)
    got_up = swap_core(sent_up)
    theirs_first, theirs_second, mine_down = grad_down_part(got_down, d_ffn)
    col_first = swap_col(theirs_first)
    if n_y == 2:
        send_theirs, send_mine, keep_theirs, keep_mine = grad_in_y(d_gate, got_gate, theirs_first)
        y_theirs = swap_y(send_theirs, 1)
        early = [col_first, y_theirs]
    else:
        theirs_gate, keep_mine = grad_in(d_gate, got_gate, theirs_first)
        early = [col_first]
    ffn_out = run(
        functools.partial(down_body, n_dp),
        ids,
        [after(hidden, keep_mine)] + downs,
        [None] * (2 + n_dp),
        [sds((rows_all, width))],
        [None],
    )[0]

    d_resid, d_low, gain_part = run(
        own_body,
        ids,
        [after(d_own, ffn_out), tokens, branch, cotangent, gains],
        [None] * 5,
        [sds((n, width), F32), sds((n, width)), sds((8, width), F32)],
        [None] * 3,
    )
    d_branch = lax.all_gather(after(d_low, *early), "row", axis=0, tiled=True)
    ffn_own = lax.psum_scatter(after(ffn_out, d_low, *early), "row", scatter_dimension=0, tiled=True)

    def y_total(value, *others):
        total = value
        step = 1
        while step < n_y:
            total = add_low(total, after(swap_y(total, step), *others))
            step *= 2
        return total

    def three(a, b, c):
        return run(three_body, ids, [a, b, c], [None] * 3, [sds(a.shape)], [None])[0]

    col_second = swap_col(after(theirs_second, col_first, d_low))
    if n_y == 2:
        y_mine = swap_y(after(send_mine, y_theirs, d_low), 1)
        theirs_gate = add_low(keep_theirs, after(y_theirs, d_low))
    col_gate = swap_col(theirs_gate)
    theirs_up, mine_up = grad_in(d_up, got_up, d_low, theirs_gate)
    sum_down = run(
        beside_body,
        ids,
        [mine_down, col_first, after(col_second, theirs_gate)],
        [None] * 3,
        [sds(mine_down.shape)],
        [None],
    )[0]
    col_up = swap_col(after(theirs_up, col_gate))
    if n_y == 2:
        moved_down = swap_y(sum_down, 1)
        sum_gate = three(keep_mine, y_mine, col_gate)
        full_gate = swap_y(sum_gate, 1)
    else:
        moved_down = sum_down
        sum_gate = add_low(keep_mine, col_gate)
        full_gate = y_total(sum_gate)

    d_query, d_kv_parts = run(
        functools.partial(attend_back_body, n_row, n_col, heads),
        ids,
        [query, kv_own, kv_oth, low_at, high_at, log_total, cos_all, sin_all]
        + [after(d_branch, sum_gate, theirs_up, sum_down), w_rows],
        [None] * 10,
        [sds((rows_all, hcols)), sds((n_row * n_col, n, 2 * HEAD))],
        [None] * 2,
        scratch=[pltpu.VMEM((rows_all, 2 * HEAD), F32)] * 2
        + [pltpu.VMEM((rows_all, hcols), BF16)],
    )
    d_kv_parts = deal(d_kv_parts, ("row", "col"))
    d_attn = run(
        attn_grad_body, ids, [after(d_query, moved_down, col_up, full_gate), w_qkv], [None] * 2, [sds((rows_all, width))], [None]
    )[0]
    d_attn_own = lax.psum_scatter(d_attn, "row", scatter_dimension=0, tiled=True)

    result = (tokens.astype(F32) + branch.astype(F32) + ffn_own.astype(F32)).astype(BF16)
    mine = lax.dynamic_slice_in_dim(result, col * half, half, 1)
    moved = swap_col(lax.dynamic_slice_in_dim(result, (1 - col) * half, half, 1))
    result = jnp.where(
        col == 0, jnp.concatenate([mine, moved], axis=0), jnp.concatenate([moved, mine], axis=0)
    )

    by_dp = width // n_dp

    def block_of(j, ids):
        return (j // 2) * 2 + ((ids[0] & 1) ^ ((j & 1) ^ 1))

    lines = n_row * n_col
    gain_lines = jnp.pad(
        gain_part[0].reshape(n_dp * lines, shard), ((0, 0), (0, used - shard))
    )
    own_cos = lax.dynamic_slice_in_dim(cos_all, row * n, n, 0)
    own_sin = lax.dynamic_slice_in_dim(sin_all, row * n, n, 0)
    d_kv = run(
        keyval_body,
        ids,
        [own_cos, own_sin, after(d_kv_parts, d_attn)],
        [None, None, None],
        [sds((n, 2 * HEAD))],
        [None],
    )[0]
    send_q, keep_q = run(
        functools.partial(project_in_body, n_row, n_col, shard),
        ids,
        [attn_in, d_query, d_kv, gain_lines],
        [
            pl.BlockSpec((rows_all, by_dp), lambda j, ids: (0, block_of(j, ids))),
            None,
            None,
            pl.BlockSpec((lines, used), lambda j, ids: (block_of(j, ids), 0)),
        ],
        [sds((around, n_row * tall, used))] * 2,
        [None] * 2,
        grid=(n_dp,),
        scratch=[pltpu.VMEM((by_dp, rows_all), BF16)],
    )
    got_q = swap_core(send_q)
    if n_y == 2:
        full_down = add_low(sum_down, after(moved_down, send_q))
        sum_up = add_low(mine_up, after(col_up, full_down))
        moved_up = swap_y(sum_up, 1)
    else:
        full_down = y_total(sum_down)
        sum_up = moved_up = add_low(mine_up, after(col_up, full_down, full_gate))
    send_o, keep_o = run(
        functools.partial(project_out_body, n_dp, n_col),
        ids,
        [mixed, after(d_branch, sum_up)],
        [None] * 2,
        [sds((around, shard, width))] * 2,
        [None] * 2,
        scratch=[pltpu.VMEM((hcols, rows_all), BF16)],
    )
    o_total = keep_o.astype(F32) + swap_core(send_o).astype(F32)
    o_total = o_total.astype(BF16)

    def parts_sum(total, *others):
        dealt = after(deal(total, ("y", "col")), *others)
        return jnp.sum(dealt.astype(F32), axis=0).astype(BF16)

    q_total = (keep_q.astype(F32) + after(got_q, full_down).astype(F32)).astype(BF16)
    def joined(mine, shape):
        return run(
            join_body,
            ids,
            [mine, swap_core(mine)],
            [None] * 2,
            [sds(shape, F32)],
            [pl.BlockSpec((shape[0] // 4, shape[1]), lambda b, ids: (b, 0))],
            grid=(4,),
        )[0]

    grad_down = joined(after(full_down, got_q), (ffn, half))
    def join_four(parts):
        return run(
            join_four_body,
            ids,
            parts + [swap_core(p) for p in parts],
            [None] * 4,
            [sds((half, ffn), F32)],
            [pl.BlockSpec((half // 4, ffn), lambda b, ids: (b, 0))],
            grid=(4,),
        )[0]

    if n_y == 2:
        grad_gate = join_four([sum_gate, after(full_gate, grad_down)])
    else:
        grad_gate = joined(full_gate, (half, ffn))

    grad_tokens = run(
        token_body,
        ids,
        [d_attn_own, d_kv, w_qkv, tokens, gains, d_resid],
        [None] * 6,
        [sds((n, width))],
        [None],
    )[0]

    q_sum = parts_sum(q_total, grad_down, grad_gate, grad_tokens, result, moved_up)
    if n_y == 2:
        full_up = add_low(sum_up, after(moved_up, q_sum))
    else:
        full_up = y_total(sum_up, q_sum)
    q_pieces = deal(q_sum.reshape(n_row, tall, used), "row")
    o_sum = parts_sum(after(o_total, q_sum))
    grad_out = transpose_devices(after(o_sum, q_pieces)).astype(F32)
    grad_up = joined(full_up, (half, ffn))
    grad_query, grad_keyval, gain_a, gain_f = run(
        functools.partial(last_body, n_row, hcols),
        ids,
        [after(q_pieces, grad_up), w_query, w_keyval, norm_attn.astype(F32)[:, None]],
        [None, None, None, None],
        [
            sds((shard, width), F32),
            sds((shard, 2 * HEAD), F32),
            sds((shard, 1), F32),
            sds((8, used), F32),
        ],
        [None] * 4,
    )
    return (
        result,
        grad_tokens,
        grad_query,
        grad_keyval,
        grad_out,
        gain_a[:, 0],
        gain_f[0, :shard],
        grad_gate,
        grad_up,
        grad_down,
    )


def solution(mesh):
    n_dp, n_row, n_col = (mesh.shape[a] for a in ("dp", "row", "col"))
    fine = jax.sharding.Mesh(mesh.devices.reshape(n_dp // 2, 2, n_row, n_col), EVERY)
    rows = P(EVERY, None)
    in_specs = (
        rows,
        rows,
        rows,
        rows,
        rows,
        P(EVERY),
        P(EVERY),
        P("col", "row"),
        P("col", "row"),
        P("row", "col"),
        P(DP, None),
        P(DP, None),
    )
    out_specs = (
        P(DP + ("row",), "col"),
        rows,
        rows,
        rows,
        rows,
        P(EVERY),
        P(EVERY),
        P("col", "row"),
        P("col", "row"),
        P("row", "col"),
    )
    return jax.shard_map(shards, mesh=fine, in_specs=in_specs, out_specs=out_specs, check_vma=False)
```

time: 2400 us -> 545 us (0.23)
  waiting for transfers between devices: 1850 us -> 210 us
  Pallas kernels: 0 us -> 172 us
  matrix products: 153 us -> 0 us
  blocking collectives: 160 us -> 54.5 us
  other arithmetic: 62.5 us -> 17.8 us
  starting transfers between devices: 90.2 us -> 47.1 us
  local copies, waits for them, and re-layouts: 55 us -> 19.8 us
    reduce_scatter x8 -> x4, waiting for transfers between devices: 1260 us -> 9.99 us  [the longest x1 9.33 us: shards(): d_own = lax.psum_scatter(d_ffn, 'row', scatter_dimension=0, tiled=True)]
    all_gather x12 -> x4, waiting for transfers between devices: 436 us -> 6.72 us  [the longest x1 5.29 us: shards(): ffn_in = lax.all_gather(ffn_own_in, 'row', axis=0, tiled=True)]
    pallas_call x0 -> x28, Pallas kernels: none -> 172 us  [run(): pl.pallas_call(body, grid_spec=pltpu.PrefetchScalarGridSpec(num_scalar_pr...]
    dot_general x26 -> x0, matrix products: 145 us -> none  [the longest x9 57 us: plain_dot(): return jnp.dot(left_side, right_side, preferred_element_type=jnp.float32)]
    unnamed x3 -> x0, blocking collectives: 125 us -> none
    ppermute x21 -> x36, waiting for transfers between devices: 72 us -> 166 us  [the longest x9 109 us: swap_col(): return lax.ppermute(value, 'col', [(0, 1), (1, 0)])]
    psum x1 -> x0, waiting for transfers between devices: 68.8 us -> none  [shards(): lax.psum(grad_both[:, :ffn_width].astype(jnp.bfloat16), 'dp')]
    ppermute x21 -> x36, starting transfers between devices: 76 us -> 26.5 us  [the longest x9 10.6 us: swap_col(): return lax.ppermute(value, 'col', [(0, 1), (1, 0)])]
  transfers between devices with their start and end apart: 45 -> 49, of which waited for: 43 -> 27; matrix products, arithmetic and copies ran while one was open for 9% -> 4% of each run, Pallas kernels for 0% -> 24%
where the time goes in v1:
time: 545 us; the launch traced here: 536 us
  waiting for transfers between devices  210 us (39%)
  Pallas kernels  172 us (32%)
  blocking collectives  54.5 us (10%)
  starting transfers between devices  47.1 us (9%)
  local copies, waits for them, and re-layouts  19.8 us (4%)
  other arithmetic  17.8 us (3%)
  between operations  15 us (3%)
    pallas_call x28, Pallas kernels, run(): pl.pallas_call(body, grid_spec=pltpu.PrefetchScalarGridSpec(num_scalar_pr...  172 us
    ppermute x9, waiting for transfers between devices, swap_col(): return lax.ppermute(value, 'col', [(0, 1), (1, 0)])  109 us
    all_to_all x2, blocking collectives, deal(): return lax.all_to_all(value, axes, split_axis=0, concat_axis=0, tiled=True)  54.5 us
    ppermute x8, waiting for transfers between devices, swap_y(): lax.ppermute(value, 'y', [(i, i ^ k) for i in range(lax.axis_size('y'))])  34 us
    all_to_all x5, waiting for transfers between devices, deal(): return lax.all_to_all(value, axes, split_axis=0, concat_axis=0, tiled=True)  25.8 us
    all_to_all x5, starting transfers between devices, deal(): return lax.all_to_all(value, axes, split_axis=0, concat_axis=0, tiled=True)  19.7 us
    ppermute x2, waiting for transfers between devices, transpose_devices(): return lax.ppermute(value, EVERY, pairs)  13.5 us
    unnamed x84, local copies, waits for them, and re-layouts  12.3 us
  transfers between devices with their start and end apart: 49, of which 27 were waited for; matrix products, arithmetic and copies ran while one was open for 4% of the time, Pallas kernels for 24%

profile of v1, /device:TPU:4, one launch (start us, length us, event | category | flops | bytes accessed | tf_op | source)
XLA Modules:
  0.0 535.9 jit_solution(18196649812518649561)
XLA Ops:
  11.0 2.4 shard_map.195
  13.5 31.0 %all_to_all.35 = bf16[4,80,768]{2,1,0:T(8,128)(2,1)S(1)} all-to-all(bf16[4,80,768]{2,1,0:T(8,128)(2,1)} %shard_map.195), channel_id=1, replica_groups=mesh['y'=2,'core'=2,'row'=4,'col'=2] {'row'}, dimensions={0} | all-to-all | bytes 983040 | tf_op jit(solution)/shard_map/all_to_all | solution.py:38
  44.7 23.5 %all_to_all.36.own_ref = bf16[4,320,768]{2,1,0:T(8,128)(2,1)S(1)} all-to-all(bf16[4,320,768]{2,1,0:T(8,128)(2,1)S(1)} %broadcast_in_dim.80), channel_id=1, replica_groups=mesh['y'=2,'core'=2,'row'=4,'col'=2] {'y','col'}, dimensions={0} | all-to-all | bytes 3932160 | tf_op jit(solution)/shard_map/all_to_all | solution.py:38
  68.2 5.1 collective-permute-start.2
  77.2 7.2 %shard_map.196 = (bf16[512,2048]{1,0:T(8,128)(2,1)}, bf16[512,256]{1,0:T(8,128)(2,1)}, bf16[512,512]{1,0:T(8,128)(2,1)}, bf16[2048,768]{1,0:T(8,128)(2,1)}, f32[8,2048]{1,0:T(8,128)}) custom-call(s32[3]{0:T(128)} %pad_add_fusion.ids, bf16[512,2048]{1,0:T(8,128)(2,1)} %all-gather.5.cloned.1.call-done.x_ref, bf16[4,320,768]{2,1,0:T(8,128)(2,1)} %copy-done.1, ...), custom_call_target="tpu_custom_call" | custom-call | bytes 100000 | tf_op jit(solution)/shard_map/pallas_call | solution.py:81
  84.3 1.8 collective-permute-done.2
  87.3 3.5 all-to-all-start.2
  93.9 15.9 %collective-permute-done.1.oth_ref.refs_2_ = bf16[512,256]{1,0:T(8,128)(2,1)S(1)} collective-permute-done((bf16[512,256]{1,0:T(8,128)(2,1)S(1)}, bf16[512,256]{1,0:T(8,128)(2,1)S(1)}, u32[]{:S(2)}, u32[]{:S(2)}) %collective-permute-start.1) | collective-permute-done | bytes 262176 | tf_op jit(solution)/shard_map/ppermute | solution.py:34
  110.5 6.2 %shard_map.197 = (bf16[512,512]{1,0:T(8,128)(2,1)}, f32[512,128]{1,0:T(8,128)}) custom-call(s32[3]{0:T(128)} %pad_add_fusion.ids, bf16[512,512]{1,0:T(8,128)(2,1)} %get-tuple-element.91.q_ref.refs_0_, bf16[512,256]{1,0:T(8,128)(2,1)} %get-tuple-element.92.own_ref.refs_1_, bf16[512,256]{1,0:T(8,128)(2,1)} %copy-done.24, ...), custom_call_target="tpu_custom_call" | custom-call | bytes 100000 | tf_op jit(solution)/shard_map/pallas_call | solution.py:81
  118.1 2.3 collective-permute-done.3.oth_ref
  121.4 5.1 shard_map.198
  126.5 3.7 shard_map.199
  130.9 19.5 %collective-permute-done.4.refs_1_ = bf16[256,1536]{1,0:T(8,128)(2,1)} collective-permute-done((bf16[256,1536]{1,0:T(8,128)(2,1)}, bf16[256,1536]{1,0:T(8,128)(2,1)}, u32[]{:S(2)}, u32[]{:S(2)}) %collective-permute-start.4) | collective-permute-done | bytes 786464 | tf_op jit(solution)/shard_map/ppermute | solution.py:34
  151.2 18.4 %collective-permute-done.5.refs_6_ = bf16[256,1536]{1,0:T(8,128)(2,1)S(1)} collective-permute-done((bf16[256,1536]{1,0:T(8,128)(2,1)}, bf16[256,1536]{1,0:T(8,128)(2,1)S(1)}, u32[]{:S(2)}, u32[]{:S(2)}) %collective-permute-start.5) | collective-permute-done | bytes 786464 | tf_op jit(solution)/shard_map/ppermute | solution.py:34
  170.7 3.0 shard_map.200
  176.0 17.1 %collective-permute-done.12.refs_11_.refs_1_ = bf16[1536,256]{1,0:T(8,128)(2,1)S(1)} collective-permute-done((bf16[1536,256]{1,0:T(8,128)(2,1)S(1)}, bf16[1536,256]{1,0:T(8,128)(2,1)S(1)}, u32[]{:S(2)}, u32[]{:S(2)}) %collective-permute-start.12) | collective-permute-done | bytes 786464 | tf_op jit(solution)/shard_map/ppermute | solution.py:34
  194.7 16.8 %collective-permute-done.14.refs_13_.refs_3_ = bf16[1536,256]{1,0:T(8,128)(2,1)S(1)} collective-permute-done((bf16[1536,256]{1,0:T(8,128)(2,1)S(1)}, bf16[1536,256]{1,0:T(8,128)(2,1)S(1)}, u32[]{:S(2)}, u32[]{:S(2)}) %collective-permute-start.14) | collective-permute-done | bytes 786464 | tf_op jit(solution)/shard_map/ppermute | solution.py:30
  212.1 1.7 collective-permute-done.11.refs_9_
  214.9 5.3 all-gather.9.cloned.1.call-done.f_ref
  220.2 33.6 %shard_map.201 = (bf16[512,1536]{1,0:T(8,128)(2,1)}, bf16[512,1536]{1,0:T(8,128)(2,1)}, bf16[512,1536]{1,0:T(8,128)(2,1)}, bf16[512,2048]{1,0:T(8,128)(2,1)}, bf...) custom-call(s32[3]{0:T(128)} %pad_add_fusion.ids, ...), custom_call_target="tpu_custom_call" | custom-call | bytes 100000 | tf_op jit(solution)/shard_map/pallas_call | solution.py:81
  254.4 5.4 %collective-permute-done.16.got_ref = bf16[2,768,1024]{2,1,0:T(8,128)(2,1)S(1)} collective-permute-done((bf16[2,768,1024]{2,1,0:T(8,128)(2,1)}, bf16[2,768,1024]{2,1,0:T(8,128)(2,1)S(1)}, u32[]{:S(2)}, u32[]{:S(2)}) %collective-permute-start.16) | collective-permute-done | bytes 3145760 | tf_op jit(solution)/shard_map/ppermute | solution.py:26
  259.8 1.7 copy-done.11
  261.4 6.8 %shard_map.202 = (bf16[768,512]{1,0:T(8,128)(2,1)}, bf16[768,512]{1,0:T(8,128)(2,1)}, bf16[768,1024]{1,0:T(8,128)(2,1)}) custom-call(s32[3]{0:T(128)} %pad_add_fusion.ids, bf16[512,1536]{1,0:T(8,128)(2,1)} %get-tuple-element.122.h_ref, bf16[512,2048]{1,0:T(8,128)(2,1)} %all-gather.7.cloned.1.call-done.c_ref, bf16[2,768,1024]{2,1,0:T(8,128)(2,1)} %copy-done.11), custom_call_target="tpu_custom_call" | custom-call | bytes 100000 | tf_op jit(solution)/shard_map/pallas_call | solution.py:81
  269.7 1.7 copy-done.10
  271.3 6.5 %shard_map.203 = (bf16[256,1536]{1,0:T(8,128)(2,1)}, bf16[256,1536]{1,0:T(8,128)(2,1)}, bf16[256,1536]{1,0:T(8,128)(2,1)}, bf16[256,1536]{1,0:T(8,128)(2,1)}) custom-call(s32[3]{0:T(128)} %pad_add_fusion.ids, bf16[512,2048]{1,0:T(8,128)(2,1)} %all-gather.9.cloned.1.call-done.f_ref, bf16[512,1536]{1,0:T(8,128)(2,1)} %get-tuple-element.119.d_ref, ...), custom_call_target="tpu_custom_call" | custom-call | bytes 100000 | tf_op jit(solution)/shard_map/pallas_call | solution.py:81
  278.4 8.7 %shard_map.204 = bf16[512,2048]{1,0:T(8,128)(2,1)} custom-call(s32[3]{0:T(128)} %pad_add_fusion.ids, bf16[512,1536]{1,0:T(8,128)(2,1)} %get-tuple-element.122.h_ref, bf16[1536,1024]{1,0:T(8,128)(2,1)} %refs_0_.3, bf16[1536,256]{1,0:T(8,128)(2,1)} %copy-done.5, bf16[1536,256]{1,0:T(8,128)(2,1)} %copy-done.7, bf16[1536,256]{1,0:T(8,128)(2,1)} %copy-done.6, ...), custom_call_target="tpu_custom_call" | custom-call | bytes 100000 | tf_op jit(solution)/shard_map/pallas_call | solution.py:81
  287.2 9.3 %reduce-scatter.7.cloned.1.call-done.d_ref = bf16[128,2048]{1,0:T(8,128)(2,1)} async-done(((bf16[512,2048]{1,0:T(8,128)(2,1)}), bf16[128,2048]{1,0:T(8,128)(2,1)}) %reduce-scatter.7.cloned.1.call-update) | async-done | bytes 524304 | tf_op jit(solution)/shard_map/reduce_scatter | solution.py:722
  296.5 4.1 shard_map.205
  301.8 1.5 collective-permute-start.24
  303.4 3.1 shard_map.206
  307.6 1.7 copy-done.9
  309.3 6.7 %shard_map.208 = (bf16[512,1536]{1,0:T(8,128)(2,1)}, bf16[512,1536]{1,0:T(8,128)(2,1)}) custom-call(s32[3]{0:T(128)} %pad_add_fusion.ids, bf16[512,2048]{1,0:T(8,128)(2,1)} %all-gather.9.cloned.1.call-done.f_ref, bf16[512,1536]{1,0:T(8,128)(2,1)} %get-tuple-element.134.d_ref, bf16[2,512,1536]{2,1,0:T(8,128)(2,1)} %copy-done.9), custom_call_target="tpu_custom_call" | custom-call | bytes 100000 | tf_op jit(solution)/shard_map/pallas_call | solution.py:81
  316.0 6.4 %collective-permute-done.24.second_ref = bf16[768,512]{1,0:T(8,128)(2,1)S(1)} collective-permute-done((bf16[768,512]{1,0:T(8,128)(2,1)}, bf16[768,512]{1,0:T(8,128)(2,1)S(1)}, u32[]{:S(2)}, u32[]{:S(2)}) %collective-permute-start.24) | collective-permute-done | bytes 786464 | tf_op jit(solution)/shard_map/ppermute | solution.py:34
  323.3 4.1 shard_map.209.left_ref
  327.9 11.0 %collective-permute-done.22.c_ref = bf16[256,1536]{1,0:T(8,128)(2,1)S(1)} collective-permute-done((bf16[256,1536]{1,0:T(8,128)(2,1)}, bf16[256,1536]{1,0:T(8,128)(2,1)S(1)}, u32[]{:S(2)}, u32[]{:S(2)}) %collective-permute-start.22) | collective-permute-done | bytes 786464 | tf_op jit(solution)/shard_map/ppermute | solution.py:34
  341.3 3.4 shard_map.207.own_ref
  346.1 11.2 %shard_map.210 = (bf16[512,512]{1,0:T(8,128)(2,1)}, bf16[8,128,256]{2,1,0:T(8,128)(2,1)}) custom-call(s32[3]{0:T(128)} %pad_add_fusion.ids, bf16[512,512]{1,0:T(8,128)(2,1)} %get-tuple-element.91.q_ref.refs_0_, bf16[512,256]{1,0:T(8,128)(2,1)} %get-tuple-element.92.own_ref.refs_1_, bf16[512,256]{1,0:T(8,128)(2,1)} %copy-done.24, ...), custom_call_target="tpu_custom_call" | custom-call | bytes 100000 | tf_op jit(solution)/shard_map/pallas_call | solution.py:81
  357.3 3.5 all-to-all-start.3
  364.1 16.7 %collective-permute-done.27.other_ref = bf16[256,1536]{1,0:T(8,128)(2,1)} collective-permute-done((bf16[256,1536]{1,0:T(8,128)(2,1)}, bf16[256,1536]{1,0:T(8,128)(2,1)}, u32[]{:S(2)}, u32[]{:S(2)}) %collective-permute-start.27) | collective-permute-done | bytes 786464 | tf_op jit(solution)/shard_map/ppermute | solution.py:30
  380.8 5.3 shard_map.211
  386.2 4.3 all-to-all-done.3.pieces_ref
  391.2 2.5 shard_map.212.dkv_ref
  393.8 7.1 %shard_map.214 = (bf16[4,320,768]{2,1,0:T(8,128)(2,1)}, bf16[4,320,768]{2,1,0:T(8,128)(2,1)}) custom-call(s32[3]{0:T(128)} %pad_add_fusion.ids, bf16[512,2048]{1,0:T(8,128)(2,1)} %get-tuple-element.150.left_ref, bf16[512,512]{1,0:T(8,128)(2,1)} %get-tuple-element.145.d_ref.dq_ref, bf16[128,256]{1,0:T(8,128)(2,1)} %shard_map.212.dkv_ref, f32[32,768]{1,0:T(8,128)} %pad.6.gain_ref), custom_call_target="tpu_custom_call" | custom-call | bytes 100000 | tf_op jit(solution)/shard_map/pallas_call | solution.py:81
  400.9 4.1 shard_map.215.mine_ref
  405.5 4.1 shard_map.218.left_ref
  410.1 5.1 shard_map.222
  415.2 1.8 add_convert_fusion
  417.0 5.1 all-to-all-start.4
  423.4 1.5 collective-permute-start.20
  424.9 5.6 %shard_map.216 = f32[1536,1024]{1,0:T(8,128)} custom-call(s32[3]{0:T(128)} %pad_add_fusion.ids, bf16[768,1024]{1,0:T(8,128)(2,1)} %shard_map.215.mine_ref, bf16[768,1024]{1,0:T(8,128)(2,1)} %collective-permute-done.29.rest_ref), custom_call_target="tpu_custom_call" | custom-call | bytes 100000 | tf_op jit(solution)/shard_map/pallas_call | solution.py:81
  431.0 20.6 %collective-permute-done.20 = bf16[128,1024]{1,0:T(8,128)(2,1)} collective-permute-done((bf16[128,1024]{1,0:T(8,128)(2,1)S(1)}, bf16[128,1024]{1,0:T(8,128)(2,1)}, u32[]{:S(2)}, u32[]{:S(2)}) %collective-permute-start.20) | collective-permute-done | bytes 262176 | tf_op jit(solution)/shard_map/ppermute | solution.py:34
  451.6 2.1 maximum_select_fusion
  453.7 2.6 add_convert_fusion.1
  456.3 4.8 shard_map.213
  461.0 5.6 %shard_map.217 = f32[1024,1536]{1,0:T(8,128)} custom-call(s32[3]{0:T(128)} %pad_add_fusion.ids, bf16[256,1536]{1,0:T(8,128)(2,1)} %shard_map.207.own_ref, bf16[256,1536]{1,0:T(8,128)(2,1)} %collective-permute-done.27.other_ref, bf16[256,1536]{1,0:T(8,128)(2,1)} %collective-permute-done.30.own_rest_ref, bf16[256,1536]{1,0:T(8,128)(2,1)} %collective-permute-done.31.other_rest_ref), custom_call_target="tpu_custom_call" | custom-call | bytes 100000 | tf_op jit(solution)/shard_map/pallas_call | solution.py:81
  468.4 4.2 all-to-all-start.6
  472.6 4.1 shard_map.219.mine_ref
  476.6 8.6 %all-to-all-done.6 = bf16[4,64,2048]{2,1,0:T(8,128)(2,1)S(1)} async-done(((bf16[4,64,2048]{2,1,0:T(8,128)(2,1)}), bf16[4,64,2048]{2,1,0:T(8,128)(2,1)S(1)}, u32[]{:S(2)}, u32[]{:S(2)}) %all-to-all-start.6) | async-done | bytes 1048608 | tf_op jit(solution)/shard_map/all_to_all | solution.py:38
  485.3 3.5 all-to-all-start.5
  488.9 12.3 %all-to-all-done.5.pieces_ref = bf16[4,80,768]{2,1,0:T(8,128)(2,1)S(1)} async-done(((bf16[4,80,768]{2,1,0:T(8,128)(2,1)}), bf16[4,80,768]{2,1,0:T(8,128)(2,1)S(1)}, u32[]{:S(2)}, u32[]{:S(2)}) %all-to-all-start.5) | async-done | bytes 491552 | tf_op jit(solution)/shard_map/all_to_all | solution.py:38
  501.2 2.3 collective-permute-start.35
  504.2 11.7 %collective-permute-done.35 = bf16[64,2048]{1,0:T(8,128)(2,1)S(1)} collective-permute-done((bf16[64,2048]{1,0:T(8,128)(2,1)S(1)}, bf16[64,2048]{1,0:T(8,128)(2,1)S(1)}, u32[]{:S(2)}, u32[]{:S(2)}) %collective-permute-start.35) | collective-permute-done | bytes 262176 | tf_op jit(solution)/shard_map/ppermute | solution.py:49
  517.9 5.6 %shard_map.220 = f32[1024,1536]{1,0:T(8,128)} custom-call(s32[3]{0:T(128)} %pad_add_fusion.ids, bf16[512,1536]{1,0:T(8,128)(2,1)} %shard_map.219.mine_ref, bf16[512,1536]{1,0:T(8,128)(2,1)} %copy-done.20), custom_call_target="tpu_custom_call" | custom-call | bytes 100000 | tf_op jit(solution)/shard_map/pallas_call | solution.py:81
  523.4 2.7 shard_map.221
  (190 shorter events, 47.6 us)
Async XLA Ops:
  7.2 70.0 %all-gather.5.cloned.1.call-start = ((), (), s32[]{:S(2)}) async-start(), calls=%async_computation.11 | async-start | bytes 2621440 | tf_op jit(solution)/shard_map/all_gather | solution.py:595
  7.9 118.6 %all-gather.7.cloned.1.call-start = ((), (), s32[]{:S(2)}) async-start(), calls=%async_computation.12 | async-start | bytes 2621440 | tf_op jit(solution)/shard_map/all_gather | solution.py:600
  44.7 23.5 %copy-start.41 = (bf16[64,2048]{1,0:T(8,128)(2,1)S(1)}, bf16[64,2048]{1,0:T(8,128)(2,1)}, u32[]{:S(2)}) copy-start(bf16[64,2048]{1,0:T(8,128)(2,1)} %param.16) | copy-start | bytes 786436
  44.7 28.7 %copy-start.36 = (s32[1,4]{1,0:T(1,128)S(1)}, s32[1,4]{1,0:T(1,128)}, u32[]{:S(2)}) copy-start(s32[1,4]{1,0:T(1,128)} %param.22) | copy-start | bytes 52
  44.7 28.7 %copy-start.37 = (s32[1,4]{1,0:T(1,128)S(1)}, s32[1,4]{1,0:T(1,128)}, u32[]{:S(2)}) copy-start(s32[1,4]{1,0:T(1,128)} %param.23) | copy-start | bytes 52
  68.2 9.0 %copy-start.1 = (bf16[4,320,768]{2,1,0:T(8,128)(2,1)}, bf16[4,320,768]{2,1,0:T(8,128)(2,1)S(1)}, u32[]{:S(2)}) copy-start(bf16[4,320,768]{2,1,0:T(8,128)(2,1)S(1)} %all_to_all.36.own_ref) | copy-start | bytes 5898244
  68.2 9.0 %collective-permute-start = (bf16[4,320,768]{2,1,0:T(8,128)(2,1)S(1)}, bf16[4,320,768]{2,1,0:T(8,128)(2,1)}, u32[]{:S(2)}, u32[]{:S(2)}) collective-permute-start(bf16[4,320,768]{2,1,0:T(8,128)(2,1)S(1)} %all_to_all.36.own_ref), channel_id=1, source_target_pairs={{0,8},{8,0},{1,9},{9,1},{2,10},{10,2},{3,11},{11,3},{4,12},{12,4},... | collective-permute-start | bytes 5898248 | tf_op jit(solution)/shard_map/ppermute | solution.py:26
  68.2 18.0 %collective-permute-start.2 = (bf16[64,2048]{1,0:T(8,128)(2,1)S(1)}, bf16[64,2048]{1,0:T(8,128)(2,1)S(1)}, u32[]{:S(2)}, u32[]{:S(2)}) collective-permute-start(bf16[64,2048]{1,0:T(8,128)(2,1)S(1)} %copy-done.41), channel_id=1, source_target_pairs={{0,0},{1,1},{2,8},{3,9},{4,16},{5,17},{6,24},{7,25},{8,2},{9,3},{1... | collective-permute-start | bytes 786440 | tf_op jit(solution)/shard_map/ppermute | solution.py:49
  87.3 29.5 %all-to-all-start.2 = ((bf16[4,64,2048]{2,1,0:T(8,128)(2,1)}), bf16[4,64,2048]{2,1,0:T(8,128)(2,1)S(1)}, u32[]{:S(2)}, u32[]{:S(2)}) async-start(bf16[4,64,2048]{2,1,0:T(8,128)(2,1)} %broadcast_in_dim.90), calls=%async_computation.2 | async-start | bytes 2097152 | tf_op jit(solution)/shard_map/all_to_all | solution.py:38
  90.8 79.9 %reduce-scatter.5.cloned.1.call-start = ((), (), s32[]{:S(2)}) async-start(), calls=%async_computation.13 | async-start | bytes 2621440 | tf_op jit(solution)/shard_map/reduce_scatter | solution.py:667
  90.8 19.0 %collective-permute-start.1 = (bf16[512,256]{1,0:T(8,128)(2,1)S(1)}, bf16[512,256]{1,0:T(8,128)(2,1)S(1)}, u32[]{:S(2)}, u32[]{:S(2)}) collective-permute-start(bf16[512,256]{1,0:T(8,128)(2,1)S(1)} %copy-done.23), channel_id=1, source_target_pairs={{0,1},{1,0},{2,3},{3,2},{4,5},{5,4},{6,7},{7,6},{8,9},{9,8},{10,11... | collective-permute-start | bytes 786440 | tf_op jit(solution)/shard_map/ppermute | solution.py:34
  92.3 17.5 %copy-start.4 = (s32[512,1]{1,0:T(8,128)}, s32[512,1]{1,0:T(8,128)S(1)}, u32[]{:S(2)}) copy-start(s32[512,1]{1,0:T(8,128)S(1)} %copy.33.hi_ref.refs_4_) | copy-start | bytes 6148
  116.8 3.6 collective-permute-start.3
  126.5 93.7 %all-gather.9.cloned.1.call-start = ((), (), s32[]{:S(2)}) async-start(), calls=%async_computation.14 | async-start | bytes 2621440 | tf_op jit(solution)/shard_map/all_gather | solution.py:676
  130.3 43.7 %copy-start.40 = (bf16[1536,256]{1,0:T(8,128)(2,1)S(1)}, bf16[1536,256]{1,0:T(8,128)(2,1)}, u32[]{:S(2)}) copy-start(bf16[1536,256]{1,0:T(8,128)(2,1)} %get-tuple-element.110) | copy-start | bytes 2359300
  130.3 20.1 %collective-permute-start.4 = (bf16[256,1536]{1,0:T(8,128)(2,1)}, bf16[256,1536]{1,0:T(8,128)(2,1)}, u32[]{:S(2)}, u32[]{:S(2)}) collective-permute-start(bf16[256,1536]{1,0:T(8,128)(2,1)} %get-tuple-element.101), channel_id=1, source_target_pairs={{0,1},{1,0},{2,3},{3,2},{4,5},{5,4},{6,7},{7,6},{8,9},{9,8},{10,11... | collective-permute-start | bytes 2359304 | tf_op jit(solution)/shard_map/ppermute | solution.py:34
  150.4 19.2 %collective-permute-start.5 = (bf16[256,1536]{1,0:T(8,128)(2,1)}, bf16[256,1536]{1,0:T(8,128)(2,1)S(1)}, u32[]{:S(2)}, u32[]{:S(2)}) collective-permute-start(bf16[256,1536]{1,0:T(8,128)(2,1)} %get-tuple-element.102), channel_id=1, source_target_pairs={{0,1},{1,0},{2,3},{3,2},{4,5},{5,4},{6,7},{7,6},{8,9},{9,8},{10,11... | collective-permute-start | bytes 2359304 | tf_op jit(solution)/shard_map/ppermute | solution.py:34
  151.0 19.0 %collective-permute-start.6 = (bf16[256,1536]{1,0:T(8,128)(2,1)}, bf16[256,1536]{1,0:T(8,128)(2,1)}, u32[]{:S(2)}, u32[]{:S(2)}) collective-permute-start(bf16[256,1536]{1,0:T(8,128)(2,1)} %collective-permute-done.4.refs_1_), channel_id=1, source_target_pairs={{0,16},{16,0},{1,17},{17,1},{2,18},{18,2},{3,19},{19,3},{4,20},{20... | collective-permute-start | bytes 2359304 | tf_op jit(solution)/shard_map/ppermute | solution.py:30
  169.6 41.8 %copy-start.25 = (bf16[256,1536]{1,0:T(8,128)(2,1)}, bf16[256,1536]{1,0:T(8,128)(2,1)S(1)}, u32[]{:S(2)}) copy-start(bf16[256,1536]{1,0:T(8,128)(2,1)S(1)} %collective-permute-done.5.refs_6_) | copy-start | bytes 2359300
  173.7 122.8 %reduce-scatter.7.cloned.1.call-start = ((), (), s32[]{:S(2)}) async-start(), calls=%async_computation.15 | async-start | bytes 2621440 | tf_op jit(solution)/shard_map/reduce_scatter | solution.py:722
  173.9 19.2 %collective-permute-start.12 = (bf16[1536,256]{1,0:T(8,128)(2,1)S(1)}, bf16[1536,256]{1,0:T(8,128)(2,1)S(1)}, u32[]{:S(2)}, u32[]{:S(2)}) collective-permute-start(bf16[1536,256]{1,0:T(8,128)(2,1)S(1)} %copy-done.40), channel_id=1, source_target_pairs={{0,1},{1,0},{2,3},{3,2},{4,5},{5,4},{6,7},{7,6},{8,9},{9,8},{10,11... | collective-permute-start | bytes 2359304 | tf_op jit(solution)/shard_map/ppermute | solution.py:34
  175.4 18.8 %collective-permute-start.10 = (bf16[256,1536]{1,0:T(8,128)(2,1)S(1)}, bf16[256,1536]{1,0:T(8,128)(2,1)S(1)}, u32[]{:S(2)}, u32[]{:S(2)}) collective-permute-start(bf16[256,1536]{1,0:T(8,128)(2,1)S(1)} %collective-permute-done.5.refs_6_), channel_id=1, source_target_pairs={{0,16},{16,0},{1,17},{17,1},{2,18},{18,2},{3,19},{19,3},{4,20},{20... | collective-permute-start | bytes 2359304 | tf_op jit(solution)/shard_map/ppermute | solution.py:30
  193.1 27.0 %copy-start.5 = (bf16[1536,256]{1,0:T(8,128)(2,1)}, bf16[1536,256]{1,0:T(8,128)(2,1)S(1)}, u32[]{:S(2)}) copy-start(bf16[1536,256]{1,0:T(8,128)(2,1)S(1)} %collective-permute-done.12.refs_11_.refs_1_) | copy-start | bytes 2359300
  193.1 18.3 %collective-permute-start.14 = (bf16[1536,256]{1,0:T(8,128)(2,1)S(1)}, bf16[1536,256]{1,0:T(8,128)(2,1)S(1)}, u32[]{:S(2)}, u32[]{:S(2)}) collective-permute-start(bf16[1536,256]{1,0:T(8,128)(2,1)S(1)} %collective-permute-done.12.refs_11_.refs_1_), channel_id=1, source_target_pairs={{0,16},{16,0},{1,17},{17,1},{2,18},{18,2},{3,19},{19,3},{4,20},{20... | collective-permute-start | bytes 2359304 | tf_op jit(solution)/shard_map/ppermute | solution.py:30
  193.7 17.8 %collective-permute-start.9 = (bf16[256,1536]{1,0:T(8,128)(2,1)S(1)}, bf16[256,1536]{1,0:T(8,128)(2,1)S(1)}, u32[]{:S(2)}, u32[]{:S(2)}) collective-permute-start(bf16[256,1536]{1,0:T(8,128)(2,1)S(1)} %collective-permute-done.5.refs_6_), channel_id=1, source_target_pairs={{0,8},{8,0},{1,9},{9,1},{2,10},{10,2},{3,11},{11,3},{4,12},{12,4},... | collective-permute-start | bytes 2359304 | tf_op jit(solution)/shard_map/ppermute | solution.py:26
  193.7 18.4 %collective-permute-start.7 = (bf16[256,1536]{1,0:T(8,128)(2,1)}, bf16[256,1536]{1,0:T(8,128)(2,1)S(1)}, u32[]{:S(2)}, u32[]{:S(2)}) collective-permute-start(bf16[256,1536]{1,0:T(8,128)(2,1)} %collective-permute-done.4.refs_1_), channel_id=1, source_target_pairs={{0,8},{8,0},{1,9},{9,1},{2,10},{10,2},{3,11},{11,3},{4,12},{12,4},... | collective-permute-start | bytes 2359304 | tf_op jit(solution)/shard_map/ppermute | solution.py:26
  194.2 17.9 %collective-permute-start.8 = (bf16[256,1536]{1,0:T(8,128)(2,1)}, bf16[256,1536]{1,0:T(8,128)(2,1)S(1)}, u32[]{:S(2)}, u32[]{:S(2)}) collective-permute-start(bf16[256,1536]{1,0:T(8,128)(2,1)} %collective-permute-done.6.refs_3_), channel_id=1, source_target_pairs={{0,8},{8,0},{1,9},{9,1},{2,10},{10,2},{3,11},{11,3},{4,12},{12,4},... | collective-permute-start | bytes 2359304 | tf_op jit(solution)/shard_map/ppermute | solution.py:26
  194.3 17.8 %copy-start.26 = (bf16[256,1536]{1,0:T(8,128)(2,1)}, bf16[256,1536]{1,0:T(8,128)(2,1)S(1)}, u32[]{:S(2)}) copy-start(bf16[256,1536]{1,0:T(8,128)(2,1)S(1)} %collective-permute-done.10.refs_8_) | copy-start | bytes 2359300
  194.3 17.8 %collective-permute-start.13 = (bf16[1536,256]{1,0:T(8,128)(2,1)S(1)}, bf16[1536,256]{1,0:T(8,128)(2,1)S(1)}, u32[]{:S(2)}, u32[]{:S(2)}) collective-permute-start(bf16[1536,256]{1,0:T(8,128)(2,1)S(1)} %collective-permute-done.12.refs_11_.refs_1_), channel_id=1, source_target_pairs={{0,8},{8,0},{1,9},{9,1},{2,10},{10,2},{3,11},{11,3},{4,12},{12,4},... | collective-permute-start | bytes 2359304 | tf_op jit(solution)/shard_map/ppermute | solution.py:26
  211.5 8.7 %copy-start.6 = (bf16[1536,256]{1,0:T(8,128)(2,1)}, bf16[1536,256]{1,0:T(8,128)(2,1)S(1)}, u32[]{:S(2)}) copy-start(bf16[1536,256]{1,0:T(8,128)(2,1)S(1)} %collective-permute-done.14.refs_13_.refs_3_) | copy-start | bytes 2359300
  211.5 2.3 collective-permute-start.11
  211.5 3.4 collective-permute-start.15
  253.8 92.3 %all-gather.11.cloned.1.call-start = ((), (), s32[]{:S(2)}) async-start(), calls=%async_computation.17 | async-start | bytes 2621440 | tf_op jit(solution)/shard_map/all_gather | solution.py:777
  253.8 5.9 %collective-permute-start.16 = (bf16[2,768,1024]{2,1,0:T(8,128)(2,1)}, bf16[2,768,1024]{2,1,0:T(8,128)(2,1)S(1)}, u32[]{:S(2)}, u32[]{:S(2)}) collective-permute-start(bf16[2,768,1024]{2,1,0:T(8,128)(2,1)} %get-tuple-element.116), channel_id=1, source_target_pairs={{0,8},{8,0},{1,9},{9,1},{2,10},{10,2},{3,11},{11,3},{4,12},{12,4},... | collective-permute-start | bytes 9437192 | tf_op jit(solution)/shard_map/ppermute | solution.py:26
  253.9 15.8 %collective-permute-start.17 = (bf16[2,512,1536]{2,1,0:T(8,128)(2,1)}, bf16[2,512,1536]{2,1,0:T(8,128)(2,1)S(1)}, u32[]{:S(2)}, u32[]{:S(2)}) collective-permute-start(bf16[2,512,1536]{2,1,0:T(8,128)(2,1)} %get-tuple-element.120), channel_id=1, source_target_pairs={{0,8},{8,0},{1,9},{9,1},{2,10},{10,2},{3,11},{11,3},{4,12},{12,4},... | collective-permute-start | bytes 9437192 | tf_op jit(solution)/shard_map/ppermute | solution.py:26
  268.2 32.4 %collective-permute-start.18 = (bf16[768,512]{1,0:T(8,128)(2,1)}, bf16[768,512]{1,0:T(8,128)(2,1)S(1)}, u32[]{:S(2)}, u32[]{:S(2)}) collective-permute-start(bf16[768,512]{1,0:T(8,128)(2,1)} %get-tuple-element.117), channel_id=1, source_target_pairs={{0,1},{1,0},{2,3},{3,2},{4,5},{5,4},{6,7},{7,6},{8,9},{9,8},{10,11... | collective-permute-start | bytes 2359304 | tf_op jit(solution)/shard_map/ppermute | solution.py:34
  277.8 22.8 %collective-permute-start.19 = (bf16[256,1536]{1,0:T(8,128)(2,1)}, bf16[256,1536]{1,0:T(8,128)(2,1)S(1)}, u32[]{:S(2)}, u32[]{:S(2)}) collective-permute-start(bf16[256,1536]{1,0:T(8,128)(2,1)} %get-tuple-element.125), channel_id=1, source_target_pairs={{0,16},{16,0},{1,17},{17,1},{2,18},{18,2},{3,19},{19,3},{4,20},{20... | collective-permute-start | bytes 2359304 | tf_op jit(solution)/shard_map/ppermute | solution.py:30
  300.7 121.3 %reduce-scatter.9.cloned.1.call-start = ((), (), s32[]{:S(2)}) async-start(), calls=%async_computation.16 | async-start | bytes 2621440 | tf_op jit(solution)/shard_map/reduce_scatter | solution.py:778
  301.8 5.9 %collective-permute-start.23 = (bf16[2,512,1536]{2,1,0:T(8,128)(2,1)}, bf16[2,512,1536]{2,1,0:T(8,128)(2,1)S(1)}, u32[]{:S(2)}, u32[]{:S(2)}) collective-permute-start(bf16[2,512,1536]{2,1,0:T(8,128)(2,1)} %get-tuple-element.135), channel_id=1, source_target_pairs={{0,8},{8,0},{1,9},{9,1},{2,10},{10,2},{3,11},{11,3},{4,12},{12,4},... | collective-permute-start | bytes 9437192 | tf_op jit(solution)/shard_map/ppermute | solution.py:26
  301.8 20.6 %collective-permute-start.24 = (bf16[768,512]{1,0:T(8,128)(2,1)}, bf16[768,512]{1,0:T(8,128)(2,1)S(1)}, u32[]{:S(2)}, u32[]{:S(2)}) collective-permute-start(bf16[768,512]{1,0:T(8,128)(2,1)} %get-tuple-element.139), channel_id=1, source_target_pairs={{0,1},{1,0},{2,3},{3,2},{4,5},{5,4},{6,7},{7,6},{8,9},{9,8},{10,11... | collective-permute-start | bytes 2359304 | tf_op jit(solution)/shard_map/ppermute | solution.py:34
  306.4 32.5 %collective-permute-start.22 = (bf16[256,1536]{1,0:T(8,128)(2,1)}, bf16[256,1536]{1,0:T(8,128)(2,1)S(1)}, u32[]{:S(2)}, u32[]{:S(2)}) collective-permute-start(bf16[256,1536]{1,0:T(8,128)(2,1)} %shard_map.206), channel_id=1, source_target_pairs={{0,1},{1,0},{2,3},{3,2},{4,5},{5,4},{6,7},{7,6},{8,9},{9,8},{10,11... | collective-permute-start | bytes 2359304 | tf_op jit(solution)/shard_map/ppermute | solution.py:34
  307.0 33.4 %collective-permute-start.21 = (bf16[256,1536]{1,0:T(8,128)(2,1)S(1)}, bf16[256,1536]{1,0:T(8,128)(2,1)S(1)}, u32[]{:S(2)}, u32[]{:S(2)}) collective-permute-start(bf16[256,1536]{1,0:T(8,128)(2,1)S(1)} %copy-done.39), channel_id=1, source_target_pairs={{0,16},{16,0},{1,17},{17,1},{2,18},{18,2},{3,19},{19,3},{4,20},{20... | collective-permute-start | bytes 2359304 | tf_op jit(solution)/shard_map/ppermute | solution.py:30
  327.4 53.4 %collective-permute-start.25 = (bf16[768,1024]{1,0:T(8,128)(2,1)}, bf16[768,1024]{1,0:T(8,128)(2,1)}, u32[]{:S(2)}, u32[]{:S(2)}) collective-permute-start(bf16[768,1024]{1,0:T(8,128)(2,1)} %shard_map.209.left_ref), channel_id=1, source_target_pairs={{0,16},{16,0},{1,17},{17,1},{2,18},{18,2},{3,19},{19,3},{4,20},{20... | collective-permute-start | bytes 4718600 | tf_op jit(solution)/shard_map/ppermute | solution.py:30
  338.9 41.9 %collective-permute-start.26 = (bf16[512,1536]{1,0:T(8,128)(2,1)}, bf16[512,1536]{1,0:T(8,128)(2,1)S(1)}, u32[]{:S(2)}, u32[]{:S(2)}) collective-permute-start(bf16[512,1536]{1,0:T(8,128)(2,1)} %get-tuple-element.144), channel_id=1, source_target_pairs={{0,1},{1,0},{2,3},{3,2},{4,5},{5,4},{6,7},{7,6},{8,9},{9,8},{10,11... | collective-permute-start | bytes 4718600 | tf_op jit(solution)/shard_map/ppermute | solution.py:34
  346.1 15.6 %copy-start.13 = (f32[512,64]{1,0:T(8,128)S(1)}, f32[512,64]{1,0:T(8,128)}, u32[]{:S(2)}) copy-start(f32[512,64]{1,0:T(8,128)} %copy-done.12) | copy-start | bytes 393220
  346.1 15.6 %copy-start.15 = (f32[512,64]{1,0:T(8,128)S(1)}, f32[512,64]{1,0:T(8,128)}, u32[]{:S(2)}) copy-start(f32[512,64]{1,0:T(8,128)} %copy-done.14) | copy-start | bytes 393220
  357.3 33.1 %all-to-all-start.3 = ((bf16[8,128,256]{2,1,0:T(8,128)(2,1)}), bf16[8,128,256]{2,1,0:T(8,128)(2,1)S(1)}, u32[]{:S(2)}, u32[]{:S(2)}) async-start(bf16[8,128,256]{2,1,0:T(8,128)(2,1)} %get-tuple-element.147), calls=%async_computation.7 | async-start | bytes 1048576 | tf_op jit(solution)/shard_map/all_to_all | solution.py:38
  360.8 95.4 %reduce-scatter.11.cloned.1.call-start = ((), (), s32[]{:S(2)}) async-start(), calls=%async_computation.18 | async-start | bytes 2621440 | tf_op jit(solution)/shard_map/reduce_scatter | solution.py:830
  361.1 19.7 %collective-permute-start.27 = (bf16[256,1536]{1,0:T(8,128)(2,1)}, bf16[256,1536]{1,0:T(8,128)(2,1)}, u32[]{:S(2)}, u32[]{:S(2)}) collective-permute-start(bf16[256,1536]{1,0:T(8,128)(2,1)} %shard_map.207.own_ref), channel_id=1, source_target_pairs={{0,16},{16,0},{1,17},{17,1},{2,18},{18,2},{3,19},{19,3},{4,20},{20... | collective-permute-start | bytes 2359304 | tf_op jit(solution)/shard_map/ppermute | solution.py:30
  400.9 4.2 collective-permute-start.28
  405.1 19.9 %collective-permute-start.29 = (bf16[768,1024]{1,0:T(8,128)(2,1)}, bf16[768,1024]{1,0:T(8,128)(2,1)}, u32[]{:S(2)}, u32[]{:S(2)}) collective-permute-start(bf16[768,1024]{1,0:T(8,128)(2,1)} %shard_map.215.mine_ref), channel_id=1, source_target_pairs={{0,8},{8,0},{1,9},{9,1},{2,10},{10,2},{3,11},{11,3},{4,12},{12,4},... | collective-permute-start | bytes 4718600 | tf_op jit(solution)/shard_map/ppermute | solution.py:26
  409.6 57.0 %collective-permute-start.32 = (bf16[512,1536]{1,0:T(8,128)(2,1)}, bf16[512,1536]{1,0:T(8,128)(2,1)}, u32[]{:S(2)}, u32[]{:S(2)}) collective-permute-start(bf16[512,1536]{1,0:T(8,128)(2,1)} %shard_map.218.left_ref), channel_id=1, source_target_pairs={{0,16},{16,0},{1,17},{17,1},{2,18},{18,2},{3,19},{19,3},{4,20},{20... | collective-permute-start | bytes 4718600 | tf_op jit(solution)/shard_map/ppermute | solution.py:30
  415.2 38.5 %collective-permute-start.34 = (bf16[4,64,2048]{2,1,0:T(8,128)(2,1)}, bf16[4,64,2048]{2,1,0:T(8,128)(2,1)}, u32[]{:S(2)}, u32[]{:S(2)}) collective-permute-start(bf16[4,64,2048]{2,1,0:T(8,128)(2,1)} %get-tuple-element.167), channel_id=1, source_target_pairs={{0,8},{8,0},{1,9},{9,1},{2,10},{10,2},{3,11},{11,3},{4,12},{12,4},... | collective-permute-start | bytes 3145736 | tf_op jit(solution)/shard_map/ppermute | solution.py:26
  417.0 50.3 %all-to-all-start.4 = ((bf16[4,320,768]{2,1,0:T(8,128)(2,1)}), bf16[4,320,768]{2,1,0:T(8,128)(2,1)S(1)}, u32[]{:S(2)}, u32[]{:S(2)}) async-start(bf16[4,320,768]{2,1,0:T(8,128)(2,1)} %add_convert_fusion), calls=%async_computation.8 | async-start | bytes 3932160 | tf_op jit(solution)/shard_map/all_to_all | solution.py:38
  423.4 30.3 %copy-start.21 = (bf16[4,64,2048]{2,1,0:T(8,128)(2,1)S(1)}, bf16[4,64,2048]{2,1,0:T(8,128)(2,1)}, u32[]{:S(2)}) copy-start(bf16[4,64,2048]{2,1,0:T(8,128)(2,1)} %get-tuple-element.166) | copy-start | bytes 3145732
  423.4 28.2 %collective-permute-start.20 = (bf16[128,1024]{1,0:T(8,128)(2,1)S(1)}, bf16[128,1024]{1,0:T(8,128)(2,1)}, u32[]{:S(2)}, u32[]{:S(2)}) collective-permute-start(bf16[128,1024]{1,0:T(8,128)(2,1)S(1)} %get-tuple-element.175), channel_id=1, source_target_pairs={{0,1},{1,0},{2,3},{3,2},{4,5},{5,4},{6,7},{7,6},{8,9},{9,8},{10,11... | collective-permute-start | bytes 786440 | tf_op jit(solution)/shard_map/ppermute | solution.py:34
  424.9 36.1 %collective-permute-start.30 = (bf16[256,1536]{1,0:T(8,128)(2,1)}, bf16[256,1536]{1,0:T(8,128)(2,1)}, u32[]{:S(2)}, u32[]{:S(2)}) collective-permute-start(bf16[256,1536]{1,0:T(8,128)(2,1)} %shard_map.207.own_ref), channel_id=1, source_target_pairs={{0,8},{8,0},{1,9},{9,1},{2,10},{10,2},{3,11},{11,3},{4,12},{12,4},... | collective-permute-start | bytes 2359304 | tf_op jit(solution)/shard_map/ppermute | solution.py:26
  430.5 30.6 %collective-permute-start.31 = (bf16[256,1536]{1,0:T(8,128)(2,1)}, bf16[256,1536]{1,0:T(8,128)(2,1)}, u32[]{:S(2)}, u32[]{:S(2)}) collective-permute-start(bf16[256,1536]{1,0:T(8,128)(2,1)} %collective-permute-done.27.other_ref), channel_id=1, source_target_pairs={{0,8},{8,0},{1,9},{9,1},{2,10},{10,2},{3,11},{11,3},{4,12},{12,4},... | collective-permute-start | bytes 2359304 | tf_op jit(solution)/shard_map/ppermute | solution.py:26
  468.4 16.8 %all-to-all-start.6 = ((bf16[4,64,2048]{2,1,0:T(8,128)(2,1)}), bf16[4,64,2048]{2,1,0:T(8,128)(2,1)S(1)}, u32[]{:S(2)}, u32[]{:S(2)}) async-start(bf16[4,64,2048]{2,1,0:T(8,128)(2,1)} %add_convert_fusion.1), calls=%async_computation.10 | async-start | bytes 2097152 | tf_op jit(solution)/shard_map/all_to_all | solution.py:38
  476.6 26.9 %copy-start.38 = (bf16[64]{0:T(256)(128)(2,1)S(1)}, bf16[64]{0:T(256)(128)(2,1)}, u32[]{:S(2)}) copy-start(bf16[64]{0:T(256)(128)(2,1)} %param.17) | copy-start | bytes 388
  476.6 40.1 %collective-permute-start.33 = (bf16[512,1536]{1,0:T(8,128)(2,1)}, bf16[512,1536]{1,0:T(8,128)(2,1)S(1)}, u32[]{:S(2)}, u32[]{:S(2)}) collective-permute-start(bf16[512,1536]{1,0:T(8,128)(2,1)} %shard_map.219.mine_ref), channel_id=1, source_target_pairs={{0,8},{8,0},{1,9},{9,1},{2,10},{10,2},{3,11},{11,3},{4,12},{12,4},... | collective-permute-start | bytes 4718600 | tf_op jit(solution)/shard_map/ppermute | solution.py:26
  485.3 16.0 %all-to-all-start.5 = ((bf16[4,80,768]{2,1,0:T(8,128)(2,1)}), bf16[4,80,768]{2,1,0:T(8,128)(2,1)S(1)}, u32[]{:S(2)}, u32[]{:S(2)}) async-start(bf16[4,80,768]{2,1,0:T(8,128)(2,1)} %bitcast.13), calls=%async_computation.9 | async-start | bytes 983040 | tf_op jit(solution)/shard_map/all_to_all | solution.py:38
  501.2 22.2 %copy-start.18 = (bf16[4,80,768]{2,1,0:T(8,128)(2,1)}, bf16[4,80,768]{2,1,0:T(8,128)(2,1)S(1)}, u32[]{:S(2)}) copy-start(bf16[4,80,768]{2,1,0:T(8,128)(2,1)S(1)} %all-to-all-done.5.pieces_ref) | copy-start | bytes 1474564
  501.2 14.7 %collective-permute-start.35 = (bf16[64,2048]{1,0:T(8,128)(2,1)S(1)}, bf16[64,2048]{1,0:T(8,128)(2,1)S(1)}, u32[]{:S(2)}, u32[]{:S(2)}) collective-permute-start(bf16[64,2048]{1,0:T(8,128)(2,1)S(1)} %reduce_sum.68), channel_id=1, source_target_pairs={{0,0},{1,1},{2,8},{3,9},{4,16},{5,17},{6,24},{7,25},{8,2},{9,3},{1... | collective-permute-start | bytes 786440 | tf_op jit(solution)/shard_map/ppermute | solution.py:49
  (27 other events, 86.7 us)
Sparse Core Ops, SparseCore 0:
  9.6 56.8 all-gather.4
  73.5 46.8 all-gather.6
  126.6 44.0 reduce-scatter.4
  173.8 46.2 all-gather.8
  253.9 42.5 reduce-scatter.6
  300.8 45.2 all-gather.10
  349.0 50.8 reduce-scatter.8
  402.3 44.7 reduce-scatter.10

commit v2 on v1

--- a/solution.py
+++ b/solution.py
@@ -888,7 +888,12 @@
         scratch=[pltpu.VMEM((hcols, rows_all), BF16)],
     )
     o_total = keep_o.astype(F32) + swap_core(send_o).astype(F32)
-    o_total = o_total.astype(BF16)
+    o_total = o_total.astype(BF16).reshape(n_y, n_col, shard, width)
+
+    def pick(value, which, axis):
+        return lax.dynamic_index_in_dim(value, which, axis, keepdims=False)
+
+    o_theirs = swap_col(pick(o_total, 1 - col, 1))
 
     def parts_sum(total, *others):
         dealt = after(deal(total, ("y", "col")), *others)
@@ -932,14 +937,18 @@
         [None],
     )[0]
 
-    q_sum = parts_sum(q_total, grad_down, grad_gate, grad_tokens, result, moved_up)
+    q_sum = parts_sum(q_total, grad_down, grad_gate, grad_tokens, result, moved_up, o_theirs)
     if n_y == 2:
         full_up = add_low(sum_up, after(moved_up, q_sum))
     else:
         full_up = y_total(sum_up, q_sum)
     q_pieces = deal(q_sum.reshape(n_row, tall, used), "row")
-    o_sum = parts_sum(after(o_total, q_sum))
-    grad_out = transpose_devices(after(o_sum, q_pieces)).astype(F32)
+    o_both = (pick(o_total, col, 1).astype(F32) + o_theirs.astype(F32)).astype(BF16)
+    y = lax.axis_index("y")
+    o_own = pick(o_both, y, 0).astype(F32)
+    for k in range(1, n_y):
+        o_own = o_own + swap_y(pick(o_both, y ^ k, 0), k).astype(F32)
+    grad_out = transpose_devices(o_own.astype(BF16)).astype(F32)
     grad_up = joined(full_up, (half, ffn))
     grad_query, grad_keyval, gain_a, gain_f = run(
         functools.partial(last_body, n_row, hcols),

time: 545 us -> 542 us (level)
    all_to_all x5 -> x4, waiting for transfers between devices: 25.8 us -> 4.27 us  [deal(): return lax.all_to_all(value, axes, split_axis=0, concat_axis=0, tiled=True)]
    ppermute x2, waiting for transfers between devices: 13.5 us -> 20.9 us  [transpose_devices(): return lax.ppermute(value, EVERY, pairs)]
    ppermute x9 -> x10, waiting for transfers between devices: 109 us -> 116 us  [swap_col(): return lax.ppermute(value, 'col', [(0, 1), (1, 0)])]
    ppermute x8 -> x9, waiting for transfers between devices: 34 us -> 38.6 us  [swap_y(): lax.ppermute(value, 'y', [(i, i ^ k) for i in range(lax.axis_size('y'))])]
    all_to_all x5 -> x4, starting transfers between devices: 19.7 us -> 15.6 us  [deal(): return lax.all_to_all(value, axes, split_axis=0, concat_axis=0, tiled=True)]
    unnamed x84 -> x88, local copies, waits for them, and re-layouts: 12.3 us -> 14 us
    ppermute x9 -> x10, starting transfers between devices: 10.6 us -> 11.1 us  [swap_col(): return lax.ppermute(value, 'col', [(0, 1), (1, 0)])]
  transfers between devices with their start and end apart: 49 -> 50, of which waited for: 27 -> 23; matrix products, arithmetic and copies ran while one was open for 4% -> 4% of each run, Pallas kernels for 24% -> 24%
where the time goes in v2:
time: 542 us; the launch traced here: 533 us
  waiting for transfers between devices  207 us (38%)
  Pallas kernels  173 us (32%)
  blocking collectives  54.8 us (10%)
  starting transfers between devices  43.8 us (8%)
  local copies, waits for them, and re-layouts  22.4 us (4%)
  other arithmetic  17.4 us (3%)
  between operations  15.1 us (3%)
    pallas_call x28, Pallas kernels, run(): pl.pallas_call(body, grid_spec=pltpu.PrefetchScalarGridSpec(num_scalar_pr...  173 us
    ppermute x10, waiting for transfers between devices, swap_col(): return lax.ppermute(value, 'col', [(0, 1), (1, 0)])  116 us
    all_to_all x2, blocking collectives, deal(): return lax.all_to_all(value, axes, split_axis=0, concat_axis=0, tiled=True)  54.8 us
    ppermute x9, waiting for transfers between devices, swap_y(): lax.ppermute(value, 'y', [(i, i ^ k) for i in range(lax.axis_size('y'))])  38.6 us
    ppermute x2, waiting for transfers between devices, transpose_devices(): return lax.ppermute(value, EVERY, pairs)  20.9 us
    all_to_all x4, starting transfers between devices, deal(): return lax.all_to_all(value, axes, split_axis=0, concat_axis=0, tiled=True)  15.6 us
    unnamed x88, local copies, waits for them, and re-layouts  14 us
    ppermute x10, starting transfers between devices, swap_col(): return lax.ppermute(value, 'col', [(0, 1), (1, 0)])  11.1 us
  transfers between devices with their start and end apart: 50, of which 23 were waited for; matrix products, arithmetic and copies ran while one was open for 4% of the time, Pallas kernels for 24%

profile of v2, /device:TPU:4, one launch (start us, length us, event | category | flops | bytes accessed | tf_op | source)
XLA Modules:
  0.0 532.7 jit_solution(4540625462811957519)
XLA Ops:
  11.1 2.4 shard_map.195
  13.6 31.0 %all_to_all.30 = bf16[4,80,768]{2,1,0:T(8,128)(2,1)S(1)} all-to-all(bf16[4,80,768]{2,1,0:T(8,128)(2,1)} %shard_map.195), channel_id=1, replica_groups=mesh['y'=2,'core'=2,'row'=4,'col'=2] {'row'}, dimensions={0} | all-to-all | bytes 983040 | tf_op jit(solution)/shard_map/all_to_all | solution.py:38
  44.8 23.8 %all_to_all.31.own_ref = bf16[4,320,768]{2,1,0:T(8,128)(2,1)S(1)} all-to-all(bf16[4,320,768]{2,1,0:T(8,128)(2,1)S(1)} %broadcast_in_dim.80), channel_id=1, replica_groups=mesh['y'=2,'core'=2,'row'=4,'col'=2] {'y','col'}, dimensions={0} | all-to-all | bytes 3932160 | tf_op jit(solution)/shard_map/all_to_all | solution.py:38
  68.5 4.9 collective-permute-start.2
  77.2 7.2 %shard_map.196 = (bf16[512,2048]{1,0:T(8,128)(2,1)}, bf16[512,256]{1,0:T(8,128)(2,1)}, bf16[512,512]{1,0:T(8,128)(2,1)}, bf16[2048,768]{1,0:T(8,128)(2,1)}, f32[8,2048]{1,0:T(8,128)}) custom-call(s32[3]{0:T(128)} %pad_add_fusion.ids, bf16[512,2048]{1,0:T(8,128)(2,1)} %all-gather.5.cloned.1.call-done.x_ref, bf16[4,320,768]{2,1,0:T(8,128)(2,1)} %copy-done.1, ...), custom_call_target="tpu_custom_call" | custom-call | bytes 100000 | tf_op jit(solution)/shard_map/pallas_call | solution.py:81
  84.4 1.8 collective-permute-done.2
  87.3 3.5 all-to-all-start.2
  94.0 15.9 %collective-permute-done.1.oth_ref.refs_2_ = bf16[512,256]{1,0:T(8,128)(2,1)S(1)} collective-permute-done((bf16[512,256]{1,0:T(8,128)(2,1)S(1)}, bf16[512,256]{1,0:T(8,128)(2,1)S(1)}, u32[]{:S(2)}, u32[]{:S(2)}) %collective-permute-start.1) | collective-permute-done | bytes 262176 | tf_op jit(solution)/shard_map/ppermute | solution.py:34
  110.6 6.2 %shard_map.197 = (bf16[512,512]{1,0:T(8,128)(2,1)}, f32[512,128]{1,0:T(8,128)}) custom-call(s32[3]{0:T(128)} %pad_add_fusion.ids, bf16[512,512]{1,0:T(8,128)(2,1)} %get-tuple-element.89.q_ref.refs_0_, bf16[512,256]{1,0:T(8,128)(2,1)} %get-tuple-element.90.own_ref.refs_1_, bf16[512,256]{1,0:T(8,128)(2,1)} %copy-done.26, ...), custom_call_target="tpu_custom_call" | custom-call | bytes 100000 | tf_op jit(solution)/shard_map/pallas_call | solution.py:81
  118.1 2.3 collective-permute-done.3.oth_ref
  121.5 5.1 shard_map.198
  126.7 3.8 shard_map.199
  131.0 19.6 %collective-permute-done.4.refs_1_ = bf16[256,1536]{1,0:T(8,128)(2,1)} collective-permute-done((bf16[256,1536]{1,0:T(8,128)(2,1)}, bf16[256,1536]{1,0:T(8,128)(2,1)}, u32[]{:S(2)}, u32[]{:S(2)}) %collective-permute-start.4) | collective-permute-done | bytes 786464 | tf_op jit(solution)/shard_map/ppermute | solution.py:34
  151.4 18.4 %collective-permute-done.5.refs_6_ = bf16[256,1536]{1,0:T(8,128)(2,1)S(1)} collective-permute-done((bf16[256,1536]{1,0:T(8,128)(2,1)}, bf16[256,1536]{1,0:T(8,128)(2,1)S(1)}, u32[]{:S(2)}, u32[]{:S(2)}) %collective-permute-start.5) | collective-permute-done | bytes 786464 | tf_op jit(solution)/shard_map/ppermute | solution.py:34
  170.8 3.0 shard_map.200
  174.0 1.5 collective-permute-start.12
  176.1 17.1 %collective-permute-done.12.refs_11_.refs_1_ = bf16[1536,256]{1,0:T(8,128)(2,1)S(1)} collective-permute-done((bf16[1536,256]{1,0:T(8,128)(2,1)S(1)}, bf16[1536,256]{1,0:T(8,128)(2,1)S(1)}, u32[]{:S(2)}, u32[]{:S(2)}) %collective-permute-start.12) | collective-permute-done | bytes 786464 | tf_op jit(solution)/shard_map/ppermute | solution.py:34
  194.8 16.7 %collective-permute-done.14.refs_13_.refs_3_ = bf16[1536,256]{1,0:T(8,128)(2,1)S(1)} collective-permute-done((bf16[1536,256]{1,0:T(8,128)(2,1)S(1)}, bf16[1536,256]{1,0:T(8,128)(2,1)S(1)}, u32[]{:S(2)}, u32[]{:S(2)}) %collective-permute-start.14) | collective-permute-done | bytes 786464 | tf_op jit(solution)/shard_map/ppermute | solution.py:30
  212.2 1.7 collective-permute-done.11.refs_9_
  215.0 5.4 %all-gather.9.cloned.1.call-done.f_ref = bf16[512,2048]{1,0:T(8,128)(2,1)} async-done(((bf16[128,2048]{1,0:T(8,128)(2,1)}), bf16[512,2048]{1,0:T(8,128)(2,1)}) %all-gather.9.cloned.1.call-update) | async-done | bytes 2097168 | tf_op jit(solution)/shard_map/all_gather | solution.py:676
  220.4 33.6 %shard_map.201 = (bf16[512,1536]{1,0:T(8,128)(2,1)}, bf16[512,1536]{1,0:T(8,128)(2,1)}, bf16[512,1536]{1,0:T(8,128)(2,1)}, bf16[512,2048]{1,0:T(8,128)(2,1)}, bf...) custom-call(s32[3]{0:T(128)} %pad_add_fusion.ids, ...), custom_call_target="tpu_custom_call" | custom-call | bytes 100000 | tf_op jit(solution)/shard_map/pallas_call | solution.py:81
  254.6 5.4 %collective-permute-done.16.got_ref = bf16[2,768,1024]{2,1,0:T(8,128)(2,1)S(1)} collective-permute-done((bf16[2,768,1024]{2,1,0:T(8,128)(2,1)}, bf16[2,768,1024]{2,1,0:T(8,128)(2,1)S(1)}, u32[]{:S(2)}, u32[]{:S(2)}) %collective-permute-start.16) | collective-permute-done | bytes 3145760 | tf_op jit(solution)/shard_map/ppermute | solution.py:26
  259.9 1.7 copy-done.13
  261.6 6.7 %shard_map.202 = (bf16[768,512]{1,0:T(8,128)(2,1)}, bf16[768,512]{1,0:T(8,128)(2,1)}, bf16[768,1024]{1,0:T(8,128)(2,1)}) custom-call(s32[3]{0:T(128)} %pad_add_fusion.ids, bf16[512,1536]{1,0:T(8,128)(2,1)} %get-tuple-element.120.h_ref, bf16[512,2048]{1,0:T(8,128)(2,1)} %all-gather.7.cloned.1.call-done.c_ref, bf16[2,768,1024]{2,1,0:T(8,128)(2,1)} %copy-done.13), custom_call_target="tpu_custom_call" | custom-call | bytes 100000 | tf_op jit(solution)/shard_map/pallas_call | solution.py:81
  268.3 1.5 collective-permute-start.18
  269.8 1.7 copy-done.12
  271.5 6.5 %shard_map.203 = (bf16[256,1536]{1,0:T(8,128)(2,1)}, bf16[256,1536]{1,0:T(8,128)(2,1)}, bf16[256,1536]{1,0:T(8,128)(2,1)}, bf16[256,1536]{1,0:T(8,128)(2,1)}) custom-call(s32[3]{0:T(128)} %pad_add_fusion.ids, bf16[512,2048]{1,0:T(8,128)(2,1)} %all-gather.9.cloned.1.call-done.f_ref, bf16[512,1536]{1,0:T(8,128)(2,1)} %get-tuple-element.117.d_ref, ...), custom_call_target="tpu_custom_call" | custom-call | bytes 100000 | tf_op jit(solution)/shard_map/pallas_call | solution.py:81
  278.5 8.8 %shard_map.204 = bf16[512,2048]{1,0:T(8,128)(2,1)} custom-call(s32[3]{0:T(128)} %pad_add_fusion.ids, bf16[512,1536]{1,0:T(8,128)(2,1)} %get-tuple-element.120.h_ref, bf16[1536,1024]{1,0:T(8,128)(2,1)} %refs_0_.3, bf16[1536,256]{1,0:T(8,128)(2,1)} %copy-done.7, bf16[1536,256]{1,0:T(8,128)(2,1)} %copy-done.9, bf16[1536,256]{1,0:T(8,128)(2,1)} %copy-done.8, ...), custom_call_target="tpu_custom_call" | custom-call | bytes 100000 | tf_op jit(solution)/shard_map/pallas_call | solution.py:81
  287.3 9.4 %reduce-scatter.7.cloned.1.call-done.d_ref = bf16[128,2048]{1,0:T(8,128)(2,1)} async-done(((bf16[512,2048]{1,0:T(8,128)(2,1)}), bf16[128,2048]{1,0:T(8,128)(2,1)}) %reduce-scatter.7.cloned.1.call-update) | async-done | bytes 524304 | tf_op jit(solution)/shard_map/reduce_scatter | solution.py:722
  296.7 4.2 shard_map.205
  302.1 1.6 collective-permute-start.24
  303.6 3.2 shard_map.206
  307.9 1.7 copy-done.11
  309.6 6.7 %shard_map.208 = (bf16[512,1536]{1,0:T(8,128)(2,1)}, bf16[512,1536]{1,0:T(8,128)(2,1)}) custom-call(s32[3]{0:T(128)} %pad_add_fusion.ids, bf16[512,2048]{1,0:T(8,128)(2,1)} %all-gather.9.cloned.1.call-done.f_ref, bf16[512,1536]{1,0:T(8,128)(2,1)} %get-tuple-element.132.d_ref, bf16[2,512,1536]{2,1,0:T(8,128)(2,1)} %copy-done.11), custom_call_target="tpu_custom_call" | custom-call | bytes 100000 | tf_op jit(solution)/shard_map/pallas_call | solution.py:81
  316.2 6.4 %collective-permute-done.24.second_ref = bf16[768,512]{1,0:T(8,128)(2,1)S(1)} collective-permute-done((bf16[768,512]{1,0:T(8,128)(2,1)}, bf16[768,512]{1,0:T(8,128)(2,1)S(1)}, u32[]{:S(2)}, u32[]{:S(2)}) %collective-permute-start.24) | collective-permute-done | bytes 786464 | tf_op jit(solution)/shard_map/ppermute | solution.py:34
  323.5 4.0 shard_map.209.left_ref
  328.2 11.0 %collective-permute-done.22.c_ref = bf16[256,1536]{1,0:T(8,128)(2,1)S(1)} collective-permute-done((bf16[256,1536]{1,0:T(8,128)(2,1)}, bf16[256,1536]{1,0:T(8,128)(2,1)S(1)}, u32[]{:S(2)}, u32[]{:S(2)}) %collective-permute-start.22) | collective-permute-done | bytes 786464 | tf_op jit(solution)/shard_map/ppermute | solution.py:34
  339.1 1.5 collective-permute-start.26
  341.5 3.5 shard_map.207.own_ref
  346.3 11.2 %shard_map.210 = (bf16[512,512]{1,0:T(8,128)(2,1)}, bf16[8,128,256]{2,1,0:T(8,128)(2,1)}) custom-call(s32[3]{0:T(128)} %pad_add_fusion.ids, bf16[512,512]{1,0:T(8,128)(2,1)} %get-tuple-element.89.q_ref.refs_0_, bf16[512,256]{1,0:T(8,128)(2,1)} %get-tuple-element.90.own_ref.refs_1_, bf16[512,256]{1,0:T(8,128)(2,1)} %copy-done.26, ...), custom_call_target="tpu_custom_call" | custom-call | bytes 100000 | tf_op jit(solution)/shard_map/pallas_call | solution.py:81
  357.6 3.5 all-to-all-start.3
  364.3 16.7 %collective-permute-done.27.other_ref = bf16[256,1536]{1,0:T(8,128)(2,1)} collective-permute-done((bf16[256,1536]{1,0:T(8,128)(2,1)}, bf16[256,1536]{1,0:T(8,128)(2,1)}, u32[]{:S(2)}, u32[]{:S(2)}) %collective-permute-start.27) | collective-permute-done | bytes 786464 | tf_op jit(solution)/shard_map/ppermute | solution.py:30
  381.0 5.4 %shard_map.211 = bf16[512,2048]{1,0:T(8,128)(2,1)} custom-call(s32[3]{0:T(128)} %pad_add_fusion.ids, bf16[512,512]{1,0:T(8,128)(2,1)} %get-tuple-element.143.d_ref.dq_ref, bf16[2048,768]{1,0:T(8,128)(2,1)} %get-tuple-element.144.w_ref.wkv_ref), custom_call_target="tpu_custom_call" | custom-call | bytes 100000 | tf_op jit(solution)/shard_map/pallas_call | solution.py:81
  386.4 4.3 all-to-all-done.3.pieces_ref
  391.5 2.5 shard_map.212.dkv_ref
  394.0 7.1 %shard_map.214 = (bf16[4,320,768]{2,1,0:T(8,128)(2,1)}, bf16[4,320,768]{2,1,0:T(8,128)(2,1)}) custom-call(s32[3]{0:T(128)} %pad_add_fusion.ids, bf16[512,2048]{1,0:T(8,128)(2,1)} %get-tuple-element.148.left_ref, bf16[512,512]{1,0:T(8,128)(2,1)} %get-tuple-element.143.d_ref.dq_ref, bf16[128,256]{1,0:T(8,128)(2,1)} %shard_map.212.dkv_ref, f32[32,768]{1,0:T(8,128)} %pad.6.gain_ref), custom_call_target="tpu_custom_call" | custom-call | bytes 100000 | tf_op jit(solution)/shard_map/pallas_call | solution.py:81
  401.1 4.1 shard_map.215.mine_ref
  405.1 4.0 shard_map.218.left_ref
  409.2 5.1 shard_map.219
  415.8 3.4 add_convert_fusion
  419.2 5.1 all-to-all-start.4
  424.4 1.6 add_convert_fusion.1
  427.8 1.5 collective-permute-start.34
  429.2 5.6 %shard_map.216 = f32[1536,1024]{1,0:T(8,128)} custom-call(s32[3]{0:T(128)} %pad_add_fusion.ids, bf16[768,1024]{1,0:T(8,128)(2,1)} %shard_map.215.mine_ref, bf16[768,1024]{1,0:T(8,128)(2,1)} %collective-permute-done.29.rest_ref), custom_call_target="tpu_custom_call" | custom-call | bytes 100000 | tf_op jit(solution)/shard_map/pallas_call | solution.py:81
  436.8 27.5 %collective-permute-done.20 = bf16[128,1024]{1,0:T(8,128)(2,1)S(1)} collective-permute-done((bf16[128,1024]{1,0:T(8,128)(2,1)S(1)}, bf16[128,1024]{1,0:T(8,128)(2,1)S(1)}, u32[]{:S(2)}, u32[]{:S(2)}) %collective-permute-start.20) | collective-permute-done | bytes 262176 | tf_op jit(solution)/shard_map/ppermute | solution.py:34
  465.3 4.8 shard_map.213
  470.0 5.6 %shard_map.217 = f32[1024,1536]{1,0:T(8,128)} custom-call(s32[3]{0:T(128)} %pad_add_fusion.ids, bf16[256,1536]{1,0:T(8,128)(2,1)} %shard_map.207.own_ref, bf16[256,1536]{1,0:T(8,128)(2,1)} %collective-permute-done.27.other_ref, bf16[256,1536]{1,0:T(8,128)(2,1)} %collective-permute-done.30.own_rest_ref, bf16[256,1536]{1,0:T(8,128)(2,1)} %collective-permute-done.31.other_rest_ref), custom_call_target="tpu_custom_call" | custom-call | bytes 100000 | tf_op jit(solution)/shard_map/pallas_call | solution.py:81
  476.8 4.2 shard_map.220.mine_ref
  481.8 3.5 all-to-all-start.5
  485.3 4.7 collective-permute-done.36
  490.0 1.9 collective-permute-start.37
  492.7 19.2 %collective-permute-done.37 = bf16[64,2048]{1,0:T(8,128)(2,1)S(1)} collective-permute-done((bf16[64,2048]{1,0:T(8,128)(2,1)S(1)}, bf16[64,2048]{1,0:T(8,128)(2,1)S(1)}, u32[]{:S(2)}, u32[]{:S(2)}) %collective-permute-start.37) | collective-permute-done | bytes 262176 | tf_op jit(solution)/shard_map/ppermute | solution.py:49
  513.9 5.6 %shard_map.221 = f32[1024,1536]{1,0:T(8,128)} custom-call(s32[3]{0:T(128)} %pad_add_fusion.ids, bf16[512,1536]{1,0:T(8,128)(2,1)} %shard_map.220.mine_ref, bf16[512,1536]{1,0:T(8,128)(2,1)} %copy-done.22), custom_call_target="tpu_custom_call" | custom-call | bytes 100000 | tf_op jit(solution)/shard_map/pallas_call | solution.py:81
  520.2 2.7 shard_map.222
  (199 shorter events, 47.1 us)
Async XLA Ops:
  7.2 70.1 %all-gather.5.cloned.1.call-start = ((), (), s32[]{:S(2)}) async-start(), calls=%async_computation.10 | async-start | bytes 2621440 | tf_op jit(solution)/shard_map/all_gather | solution.py:595
  7.9 118.7 %all-gather.7.cloned.1.call-start = ((), (), s32[]{:S(2)}) async-start(), calls=%async_computation.11 | async-start | bytes 2621440 | tf_op jit(solution)/shard_map/all_gather | solution.py:600
  44.7 23.8 %copy-start.43 = (bf16[64,2048]{1,0:T(8,128)(2,1)S(1)}, bf16[64,2048]{1,0:T(8,128)(2,1)}, u32[]{:S(2)}) copy-start(bf16[64,2048]{1,0:T(8,128)(2,1)} %param.16) | copy-start | bytes 786436
  44.7 28.7 %copy-start.38 = (s32[1,4]{1,0:T(1,128)S(1)}, s32[1,4]{1,0:T(1,128)}, u32[]{:S(2)}) copy-start(s32[1,4]{1,0:T(1,128)} %param.22) | copy-start | bytes 52
  44.8 28.7 %copy-start.39 = (s32[1,4]{1,0:T(1,128)S(1)}, s32[1,4]{1,0:T(1,128)}, u32[]{:S(2)}) copy-start(s32[1,4]{1,0:T(1,128)} %param.23) | copy-start | bytes 52
  68.5 8.7 %copy-start.1 = (bf16[4,320,768]{2,1,0:T(8,128)(2,1)}, bf16[4,320,768]{2,1,0:T(8,128)(2,1)S(1)}, u32[]{:S(2)}) copy-start(bf16[4,320,768]{2,1,0:T(8,128)(2,1)S(1)} %all_to_all.31.own_ref) | copy-start | bytes 5898244
  68.5 8.7 %collective-permute-start = (bf16[4,320,768]{2,1,0:T(8,128)(2,1)S(1)}, bf16[4,320,768]{2,1,0:T(8,128)(2,1)}, u32[]{:S(2)}, u32[]{:S(2)}) collective-permute-start(bf16[4,320,768]{2,1,0:T(8,128)(2,1)S(1)} %all_to_all.31.own_ref), channel_id=1, source_target_pairs={{0,8},{8,0},{1,9},{9,1},{2,10},{10,2},{3,11},{11,3},{4,12},{12,4},... | collective-permute-start | bytes 5898248 | tf_op jit(solution)/shard_map/ppermute | solution.py:26
  68.5 17.6 %collective-permute-start.2 = (bf16[64,2048]{1,0:T(8,128)(2,1)S(1)}, bf16[64,2048]{1,0:T(8,128)(2,1)S(1)}, u32[]{:S(2)}, u32[]{:S(2)}) collective-permute-start(bf16[64,2048]{1,0:T(8,128)(2,1)S(1)} %copy-done.43), channel_id=1, source_target_pairs={{0,0},{1,1},{2,8},{3,9},{4,16},{5,17},{6,24},{7,25},{8,2},{9,3},{1... | collective-permute-start | bytes 786440 | tf_op jit(solution)/shard_map/ppermute | solution.py:49
  76.2 8.2 %copy-start.14 = (f32[512,64]{1,0:T(8,128)}, f32[512,64]{1,0:T(8,128)S(1)}, u32[]{:S(2)}) copy-start(f32[512,64]{1,0:T(8,128)S(1)} %get-tuple-element.173) | copy-start | bytes 393220
  87.3 29.6 %all-to-all-start.2 = ((bf16[4,64,2048]{2,1,0:T(8,128)(2,1)}), bf16[4,64,2048]{2,1,0:T(8,128)(2,1)S(1)}, u32[]{:S(2)}, u32[]{:S(2)}) async-start(bf16[4,64,2048]{2,1,0:T(8,128)(2,1)} %broadcast_in_dim.90), calls=%async_computation.2 | async-start | bytes 2097152 | tf_op jit(solution)/shard_map/all_to_all | solution.py:38
  90.8 80.0 %reduce-scatter.5.cloned.1.call-start = ((), (), s32[]{:S(2)}) async-start(), calls=%async_computation.12 | async-start | bytes 2621440 | tf_op jit(solution)/shard_map/reduce_scatter | solution.py:667
  90.9 19.0 %collective-permute-start.1 = (bf16[512,256]{1,0:T(8,128)(2,1)S(1)}, bf16[512,256]{1,0:T(8,128)(2,1)S(1)}, u32[]{:S(2)}, u32[]{:S(2)}) collective-permute-start(bf16[512,256]{1,0:T(8,128)(2,1)S(1)} %copy-done.25), channel_id=1, source_target_pairs={{0,1},{1,0},{2,3},{3,2},{4,5},{5,4},{6,7},{7,6},{8,9},{9,8},{10,11... | collective-permute-start | bytes 786440 | tf_op jit(solution)/shard_map/ppermute | solution.py:34
  92.4 17.5 %copy-start.6 = (s32[512,1]{1,0:T(8,128)}, s32[512,1]{1,0:T(8,128)S(1)}, u32[]{:S(2)}) copy-start(s32[512,1]{1,0:T(8,128)S(1)} %copy.35.hi_ref.refs_4_) | copy-start | bytes 6148
  116.8 3.6 collective-permute-start.3
  126.6 93.7 %all-gather.9.cloned.1.call-start = ((), (), s32[]{:S(2)}) async-start(), calls=%async_computation.13 | async-start | bytes 2621440 | tf_op jit(solution)/shard_map/all_gather | solution.py:676
  130.5 43.6 %copy-start.42 = (bf16[1536,256]{1,0:T(8,128)(2,1)S(1)}, bf16[1536,256]{1,0:T(8,128)(2,1)}, u32[]{:S(2)}) copy-start(bf16[1536,256]{1,0:T(8,128)(2,1)} %get-tuple-element.108) | copy-start | bytes 2359300
  130.5 20.1 %collective-permute-start.4 = (bf16[256,1536]{1,0:T(8,128)(2,1)}, bf16[256,1536]{1,0:T(8,128)(2,1)}, u32[]{:S(2)}, u32[]{:S(2)}) collective-permute-start(bf16[256,1536]{1,0:T(8,128)(2,1)} %get-tuple-element.99), channel_id=1, source_target_pairs={{0,1},{1,0},{2,3},{3,2},{4,5},{5,4},{6,7},{7,6},{8,9},{9,8},{10,11... | collective-permute-start | bytes 2359304 | tf_op jit(solution)/shard_map/ppermute | solution.py:34
  150.6 19.2 %collective-permute-start.5 = (bf16[256,1536]{1,0:T(8,128)(2,1)}, bf16[256,1536]{1,0:T(8,128)(2,1)S(1)}, u32[]{:S(2)}, u32[]{:S(2)}) collective-permute-start(bf16[256,1536]{1,0:T(8,128)(2,1)} %get-tuple-element.100), channel_id=1, source_target_pairs={{0,1},{1,0},{2,3},{3,2},{4,5},{5,4},{6,7},{7,6},{8,9},{9,8},{10,11... | collective-permute-start | bytes 2359304 | tf_op jit(solution)/shard_map/ppermute | solution.py:34
  151.1 19.0 %collective-permute-start.6 = (bf16[256,1536]{1,0:T(8,128)(2,1)}, bf16[256,1536]{1,0:T(8,128)(2,1)}, u32[]{:S(2)}, u32[]{:S(2)}) collective-permute-start(bf16[256,1536]{1,0:T(8,128)(2,1)} %collective-permute-done.4.refs_1_), channel_id=1, source_target_pairs={{0,16},{16,0},{1,17},{17,1},{2,18},{18,2},{3,19},{19,3},{4,20},{20... | collective-permute-start | bytes 2359304 | tf_op jit(solution)/shard_map/ppermute | solution.py:30
  169.8 41.7 %copy-start.27 = (bf16[256,1536]{1,0:T(8,128)(2,1)}, bf16[256,1536]{1,0:T(8,128)(2,1)S(1)}, u32[]{:S(2)}) copy-start(bf16[256,1536]{1,0:T(8,128)(2,1)S(1)} %collective-permute-done.5.refs_6_) | copy-start | bytes 2359300
  173.8 122.9 %reduce-scatter.7.cloned.1.call-start = ((), (), s32[]{:S(2)}) async-start(), calls=%async_computation.14 | async-start | bytes 2621440 | tf_op jit(solution)/shard_map/reduce_scatter | solution.py:722
  174.0 19.2 %collective-permute-start.12 = (bf16[1536,256]{1,0:T(8,128)(2,1)S(1)}, bf16[1536,256]{1,0:T(8,128)(2,1)S(1)}, u32[]{:S(2)}, u32[]{:S(2)}) collective-permute-start(bf16[1536,256]{1,0:T(8,128)(2,1)S(1)} %copy-done.42), channel_id=1, source_target_pairs={{0,1},{1,0},{2,3},{3,2},{4,5},{5,4},{6,7},{7,6},{8,9},{9,8},{10,11... | collective-permute-start | bytes 2359304 | tf_op jit(solution)/shard_map/ppermute | solution.py:34
  175.6 18.8 %collective-permute-start.10 = (bf16[256,1536]{1,0:T(8,128)(2,1)S(1)}, bf16[256,1536]{1,0:T(8,128)(2,1)S(1)}, u32[]{:S(2)}, u32[]{:S(2)}) collective-permute-start(bf16[256,1536]{1,0:T(8,128)(2,1)S(1)} %collective-permute-done.5.refs_6_), channel_id=1, source_target_pairs={{0,16},{16,0},{1,17},{17,1},{2,18},{18,2},{3,19},{19,3},{4,20},{20... | collective-permute-start | bytes 2359304 | tf_op jit(solution)/shard_map/ppermute | solution.py:30
  193.2 27.1 %copy-start.7 = (bf16[1536,256]{1,0:T(8,128)(2,1)}, bf16[1536,256]{1,0:T(8,128)(2,1)S(1)}, u32[]{:S(2)}) copy-start(bf16[1536,256]{1,0:T(8,128)(2,1)S(1)} %collective-permute-done.12.refs_11_.refs_1_) | copy-start | bytes 2359300
  193.2 18.3 %collective-permute-start.14 = (bf16[1536,256]{1,0:T(8,128)(2,1)S(1)}, bf16[1536,256]{1,0:T(8,128)(2,1)S(1)}, u32[]{:S(2)}, u32[]{:S(2)}) collective-permute-start(bf16[1536,256]{1,0:T(8,128)(2,1)S(1)} %collective-permute-done.12.refs_11_.refs_1_), channel_id=1, source_target_pairs={{0,16},{16,0},{1,17},{17,1},{2,18},{18,2},{3,19},{19,3},{4,20},{20... | collective-permute-start | bytes 2359304 | tf_op jit(solution)/shard_map/ppermute | solution.py:30
  193.8 17.8 %collective-permute-start.9 = (bf16[256,1536]{1,0:T(8,128)(2,1)S(1)}, bf16[256,1536]{1,0:T(8,128)(2,1)S(1)}, u32[]{:S(2)}, u32[]{:S(2)}) collective-permute-start(bf16[256,1536]{1,0:T(8,128)(2,1)S(1)} %collective-permute-done.5.refs_6_), channel_id=1, source_target_pairs={{0,8},{8,0},{1,9},{9,1},{2,10},{10,2},{3,11},{11,3},{4,12},{12,4},... | collective-permute-start | bytes 2359304 | tf_op jit(solution)/shard_map/ppermute | solution.py:26
  193.8 18.4 %collective-permute-start.7 = (bf16[256,1536]{1,0:T(8,128)(2,1)}, bf16[256,1536]{1,0:T(8,128)(2,1)S(1)}, u32[]{:S(2)}, u32[]{:S(2)}) collective-permute-start(bf16[256,1536]{1,0:T(8,128)(2,1)} %collective-permute-done.4.refs_1_), channel_id=1, source_target_pairs={{0,8},{8,0},{1,9},{9,1},{2,10},{10,2},{3,11},{11,3},{4,12},{12,4},... | collective-permute-start | bytes 2359304 | tf_op jit(solution)/shard_map/ppermute | solution.py:26
  194.3 17.9 %collective-permute-start.8 = (bf16[256,1536]{1,0:T(8,128)(2,1)}, bf16[256,1536]{1,0:T(8,128)(2,1)S(1)}, u32[]{:S(2)}, u32[]{:S(2)}) collective-permute-start(bf16[256,1536]{1,0:T(8,128)(2,1)} %collective-permute-done.6.refs_3_), channel_id=1, source_target_pairs={{0,8},{8,0},{1,9},{9,1},{2,10},{10,2},{3,11},{11,3},{4,12},{12,4},... | collective-permute-start | bytes 2359304 | tf_op jit(solution)/shard_map/ppermute | solution.py:26
  194.4 17.8 %copy-start.28 = (bf16[256,1536]{1,0:T(8,128)(2,1)}, bf16[256,1536]{1,0:T(8,128)(2,1)S(1)}, u32[]{:S(2)}) copy-start(bf16[256,1536]{1,0:T(8,128)(2,1)S(1)} %collective-permute-done.10.refs_8_) | copy-start | bytes 2359300
  194.4 17.8 %collective-permute-start.13 = (bf16[1536,256]{1,0:T(8,128)(2,1)S(1)}, bf16[1536,256]{1,0:T(8,128)(2,1)S(1)}, u32[]{:S(2)}, u32[]{:S(2)}) collective-permute-start(bf16[1536,256]{1,0:T(8,128)(2,1)S(1)} %collective-permute-done.12.refs_11_.refs_1_), channel_id=1, source_target_pairs={{0,8},{8,0},{1,9},{9,1},{2,10},{10,2},{3,11},{11,3},{4,12},{12,4},... | collective-permute-start | bytes 2359304 | tf_op jit(solution)/shard_map/ppermute | solution.py:26
  211.6 8.8 %copy-start.8 = (bf16[1536,256]{1,0:T(8,128)(2,1)}, bf16[1536,256]{1,0:T(8,128)(2,1)S(1)}, u32[]{:S(2)}) copy-start(bf16[1536,256]{1,0:T(8,128)(2,1)S(1)} %collective-permute-done.14.refs_13_.refs_3_) | copy-start | bytes 2359300
  211.6 2.3 collective-permute-start.11
  211.6 3.4 collective-permute-start.15
  253.9 92.4 %all-gather.11.cloned.1.call-start = ((), (), s32[]{:S(2)}) async-start(), calls=%async_computation.16 | async-start | bytes 2621440 | tf_op jit(solution)/shard_map/all_gather | solution.py:777
  254.0 5.9 %collective-permute-start.16 = (bf16[2,768,1024]{2,1,0:T(8,128)(2,1)}, bf16[2,768,1024]{2,1,0:T(8,128)(2,1)S(1)}, u32[]{:S(2)}, u32[]{:S(2)}) collective-permute-start(bf16[2,768,1024]{2,1,0:T(8,128)(2,1)} %get-tuple-element.114), channel_id=1, source_target_pairs={{0,8},{8,0},{1,9},{9,1},{2,10},{10,2},{3,11},{11,3},{4,12},{12,4},... | collective-permute-start | bytes 9437192 | tf_op jit(solution)/shard_map/ppermute | solution.py:26
  254.1 15.7 %collective-permute-start.17 = (bf16[2,512,1536]{2,1,0:T(8,128)(2,1)}, bf16[2,512,1536]{2,1,0:T(8,128)(2,1)S(1)}, u32[]{:S(2)}, u32[]{:S(2)}) collective-permute-start(bf16[2,512,1536]{2,1,0:T(8,128)(2,1)} %get-tuple-element.118), channel_id=1, source_target_pairs={{0,8},{8,0},{1,9},{9,1},{2,10},{10,2},{3,11},{11,3},{4,12},{12,4},... | collective-permute-start | bytes 9437192 | tf_op jit(solution)/shard_map/ppermute | solution.py:26
  268.3 32.5 %collective-permute-start.18 = (bf16[768,512]{1,0:T(8,128)(2,1)}, bf16[768,512]{1,0:T(8,128)(2,1)S(1)}, u32[]{:S(2)}, u32[]{:S(2)}) collective-permute-start(bf16[768,512]{1,0:T(8,128)(2,1)} %get-tuple-element.115), channel_id=1, source_target_pairs={{0,1},{1,0},{2,3},{3,2},{4,5},{5,4},{6,7},{7,6},{8,9},{9,8},{10,11... | collective-permute-start | bytes 2359304 | tf_op jit(solution)/shard_map/ppermute | solution.py:34
  277.9 22.9 %collective-permute-start.19 = (bf16[256,1536]{1,0:T(8,128)(2,1)}, bf16[256,1536]{1,0:T(8,128)(2,1)S(1)}, u32[]{:S(2)}, u32[]{:S(2)}) collective-permute-start(bf16[256,1536]{1,0:T(8,128)(2,1)} %get-tuple-element.123), channel_id=1, source_target_pairs={{0,16},{16,0},{1,17},{17,1},{2,18},{18,2},{3,19},{19,3},{4,20},{20... | collective-permute-start | bytes 2359304 | tf_op jit(solution)/shard_map/ppermute | solution.py:30
  300.9 133.9 %reduce-scatter.9.cloned.1.call-start = ((), (), s32[]{:S(2)}) async-start(), calls=%async_computation.15 | async-start | bytes 2621440 | tf_op jit(solution)/shard_map/reduce_scatter | solution.py:778
  302.0 5.9 %collective-permute-start.23 = (bf16[2,512,1536]{2,1,0:T(8,128)(2,1)}, bf16[2,512,1536]{2,1,0:T(8,128)(2,1)S(1)}, u32[]{:S(2)}, u32[]{:S(2)}) collective-permute-start(bf16[2,512,1536]{2,1,0:T(8,128)(2,1)} %get-tuple-element.133), channel_id=1, source_target_pairs={{0,8},{8,0},{1,9},{9,1},{2,10},{10,2},{3,11},{11,3},{4,12},{12,4},... | collective-permute-start | bytes 9437192 | tf_op jit(solution)/shard_map/ppermute | solution.py:26
  302.1 20.6 %collective-permute-start.24 = (bf16[768,512]{1,0:T(8,128)(2,1)}, bf16[768,512]{1,0:T(8,128)(2,1)S(1)}, u32[]{:S(2)}, u32[]{:S(2)}) collective-permute-start(bf16[768,512]{1,0:T(8,128)(2,1)} %get-tuple-element.137), channel_id=1, source_target_pairs={{0,1},{1,0},{2,3},{3,2},{4,5},{5,4},{6,7},{7,6},{8,9},{9,8},{10,11... | collective-permute-start | bytes 2359304 | tf_op jit(solution)/shard_map/ppermute | solution.py:34
  306.8 32.3 %collective-permute-start.22 = (bf16[256,1536]{1,0:T(8,128)(2,1)}, bf16[256,1536]{1,0:T(8,128)(2,1)S(1)}, u32[]{:S(2)}, u32[]{:S(2)}) collective-permute-start(bf16[256,1536]{1,0:T(8,128)(2,1)} %shard_map.206), channel_id=1, source_target_pairs={{0,1},{1,0},{2,3},{3,2},{4,5},{5,4},{6,7},{7,6},{8,9},{9,8},{10,11... | collective-permute-start | bytes 2359304 | tf_op jit(solution)/shard_map/ppermute | solution.py:34
  307.3 33.3 %collective-permute-start.21 = (bf16[256,1536]{1,0:T(8,128)(2,1)S(1)}, bf16[256,1536]{1,0:T(8,128)(2,1)S(1)}, u32[]{:S(2)}, u32[]{:S(2)}) collective-permute-start(bf16[256,1536]{1,0:T(8,128)(2,1)S(1)} %copy-done.41), channel_id=1, source_target_pairs={{0,16},{16,0},{1,17},{17,1},{2,18},{18,2},{3,19},{19,3},{4,20},{20... | collective-permute-start | bytes 2359304 | tf_op jit(solution)/shard_map/ppermute | solution.py:30
  327.6 53.4 %collective-permute-start.25 = (bf16[768,1024]{1,0:T(8,128)(2,1)}, bf16[768,1024]{1,0:T(8,128)(2,1)S(1)}, u32[]{:S(2)}, u32[]{:S(2)}) collective-permute-start(bf16[768,1024]{1,0:T(8,128)(2,1)} %shard_map.209.left_ref), channel_id=1, source_target_pairs={{0,16},{16,0},{1,17},{17,1},{2,18},{18,2},{3,19},{19,3},{4,20},{20... | collective-permute-start | bytes 4718600 | tf_op jit(solution)/shard_map/ppermute | solution.py:30
  339.1 41.9 %collective-permute-start.26 = (bf16[512,1536]{1,0:T(8,128)(2,1)}, bf16[512,1536]{1,0:T(8,128)(2,1)}, u32[]{:S(2)}, u32[]{:S(2)}) collective-permute-start(bf16[512,1536]{1,0:T(8,128)(2,1)} %get-tuple-element.142), channel_id=1, source_target_pairs={{0,1},{1,0},{2,3},{3,2},{4,5},{5,4},{6,7},{7,6},{8,9},{9,8},{10,11... | collective-permute-start | bytes 4718600 | tf_op jit(solution)/shard_map/ppermute | solution.py:34
  346.3 15.6 %copy-start.15 = (f32[512,64]{1,0:T(8,128)S(1)}, f32[512,64]{1,0:T(8,128)}, u32[]{:S(2)}) copy-start(f32[512,64]{1,0:T(8,128)} %copy-done.14) | copy-start | bytes 393220
  346.3 15.6 %copy-start.17 = (f32[512,64]{1,0:T(8,128)S(1)}, f32[512,64]{1,0:T(8,128)}, u32[]{:S(2)}) copy-start(f32[512,64]{1,0:T(8,128)} %copy-done.16) | copy-start | bytes 393220
  357.6 33.1 %all-to-all-start.3 = ((bf16[8,128,256]{2,1,0:T(8,128)(2,1)}), bf16[8,128,256]{2,1,0:T(8,128)(2,1)S(1)}, u32[]{:S(2)}, u32[]{:S(2)}) async-start(bf16[8,128,256]{2,1,0:T(8,128)(2,1)} %get-tuple-element.145), calls=%async_computation.7 | async-start | bytes 1048576 | tf_op jit(solution)/shard_map/all_to_all | solution.py:38
  361.1 104.2 %reduce-scatter.11.cloned.1.call-start = ((), (), s32[]{:S(2)}) async-start(), calls=%async_computation.17 | async-start | bytes 2621440 | tf_op jit(solution)/shard_map/reduce_scatter | solution.py:830
  361.4 19.7 %collective-permute-start.27 = (bf16[256,1536]{1,0:T(8,128)(2,1)}, bf16[256,1536]{1,0:T(8,128)(2,1)}, u32[]{:S(2)}, u32[]{:S(2)}) collective-permute-start(bf16[256,1536]{1,0:T(8,128)(2,1)} %shard_map.207.own_ref), channel_id=1, source_target_pairs={{0,16},{16,0},{1,17},{17,1},{2,18},{18,2},{3,19},{19,3},{4,20},{20... | collective-permute-start | bytes 2359304 | tf_op jit(solution)/shard_map/ppermute | solution.py:30
  401.1 13.7 %collective-permute-start.28 = (bf16[4,320,768]{2,1,0:T(8,128)(2,1)}, bf16[4,320,768]{2,1,0:T(8,128)(2,1)}, u32[]{:S(2)}, u32[]{:S(2)}) collective-permute-start(bf16[4,320,768]{2,1,0:T(8,128)(2,1)} %get-tuple-element.151), channel_id=1, source_target_pairs={{0,8},{8,0},{1,9},{9,1},{2,10},{10,2},{3,11},{11,3},{4,12},{12,4},... | collective-permute-start | bytes 5898248 | tf_op jit(solution)/shard_map/ppermute | solution.py:26
  414.3 10.1 %collective-permute-start.33 = (bf16[4,64,2048]{2,1,0:T(8,128)(2,1)}, bf16[4,64,2048]{2,1,0:T(8,128)(2,1)}, u32[]{:S(2)}, u32[]{:S(2)}) collective-permute-start(bf16[4,64,2048]{2,1,0:T(8,128)(2,1)} %get-tuple-element.160), channel_id=1, source_target_pairs={{0,8},{8,0},{1,9},{9,1},{2,10},{10,2},{3,11},{11,3},{4,12},{12,4},... | collective-permute-start | bytes 3145736 | tf_op jit(solution)/shard_map/ppermute | solution.py:26
  414.7 14.5 %collective-permute-start.29 = (bf16[768,1024]{1,0:T(8,128)(2,1)}, bf16[768,1024]{1,0:T(8,128)(2,1)}, u32[]{:S(2)}, u32[]{:S(2)}) collective-permute-start(bf16[768,1024]{1,0:T(8,128)(2,1)} %shard_map.215.mine_ref), channel_id=1, source_target_pairs={{0,8},{8,0},{1,9},{9,1},{2,10},{10,2},{3,11},{11,3},{4,12},{12,4},... | collective-permute-start | bytes 4718600 | tf_op jit(solution)/shard_map/ppermute | solution.py:26
  414.8 55.2 %collective-permute-start.30 = (bf16[256,1536]{1,0:T(8,128)(2,1)}, bf16[256,1536]{1,0:T(8,128)(2,1)}, u32[]{:S(2)}, u32[]{:S(2)}) collective-permute-start(bf16[256,1536]{1,0:T(8,128)(2,1)} %shard_map.207.own_ref), channel_id=1, source_target_pairs={{0,8},{8,0},{1,9},{9,1},{2,10},{10,2},{3,11},{11,3},{4,12},{12,4},... | collective-permute-start | bytes 2359304 | tf_op jit(solution)/shard_map/ppermute | solution.py:26
  415.2 60.4 %collective-permute-start.32 = (bf16[512,1536]{1,0:T(8,128)(2,1)}, bf16[512,1536]{1,0:T(8,128)(2,1)}, u32[]{:S(2)}, u32[]{:S(2)}) collective-permute-start(bf16[512,1536]{1,0:T(8,128)(2,1)} %shard_map.218.left_ref), channel_id=1, source_target_pairs={{0,16},{16,0},{1,17},{17,1},{2,18},{18,2},{3,19},{19,3},{4,20},{20... | collective-permute-start | bytes 4718600 | tf_op jit(solution)/shard_map/ppermute | solution.py:30
  419.2 56.4 %all-to-all-start.4 = ((bf16[4,320,768]{2,1,0:T(8,128)(2,1)}), bf16[4,320,768]{2,1,0:T(8,128)(2,1)S(1)}, u32[]{:S(2)}, u32[]{:S(2)}) async-start(bf16[4,320,768]{2,1,0:T(8,128)(2,1)} %add_convert_fusion), calls=%async_computation.8 | async-start | bytes 3932160 | tf_op jit(solution)/shard_map/all_to_all | solution.py:38
  427.8 47.8 %collective-permute-start.34 = (bf16[2,64,2048]{2,1,0:T(8,128)(2,1)}, bf16[2,64,2048]{2,1,0:T(8,128)(2,1)S(1)}, u32[]{:S(2)}, u32[]{:S(2)}) collective-permute-start(bf16[2,64,2048]{2,1,0:T(8,128)(2,1)} %dynamic-slice_bitcast_fusion), channel_id=1, source_target_pairs={{0,1},{1,0},{2,3},{3,2},{4,5},{5,4},{6,7},{7,6},{8,9},{9,8},{10,11... | collective-permute-start | bytes 1572872 | tf_op jit(solution)/shard_map/ppermute | solution.py:34
  434.9 35.2 %collective-permute-start.31 = (bf16[256,1536]{1,0:T(8,128)(2,1)}, bf16[256,1536]{1,0:T(8,128)(2,1)}, u32[]{:S(2)}, u32[]{:S(2)}) collective-permute-start(bf16[256,1536]{1,0:T(8,128)(2,1)} %collective-permute-done.27.other_ref), channel_id=1, source_target_pairs={{0,8},{8,0},{1,9},{9,1},{2,10},{10,2},{3,11},{11,3},{4,12},{12,4},... | collective-permute-start | bytes 2359304 | tf_op jit(solution)/shard_map/ppermute | solution.py:26
  436.2 28.1 %collective-permute-start.20 = (bf16[128,1024]{1,0:T(8,128)(2,1)S(1)}, bf16[128,1024]{1,0:T(8,128)(2,1)S(1)}, u32[]{:S(2)}, u32[]{:S(2)}) collective-permute-start(bf16[128,1024]{1,0:T(8,128)(2,1)S(1)} %get-tuple-element.171), channel_id=1, source_target_pairs={{0,1},{1,0},{2,3},{3,2},{4,5},{5,4},{6,7},{7,6},{8,9},{9,8},{10,11... | collective-permute-start | bytes 786440 | tf_op jit(solution)/shard_map/ppermute | solution.py:34
  481.0 11.0 %copy-start.40 = (bf16[64]{0:T(256)(128)(2,1)S(1)}, bf16[64]{0:T(256)(128)(2,1)}, u32[]{:S(2)}) copy-start(bf16[64]{0:T(256)(128)(2,1)} %param.17) | copy-start | bytes 388
  481.0 31.7 %collective-permute-start.35 = (bf16[512,1536]{1,0:T(8,128)(2,1)}, bf16[512,1536]{1,0:T(8,128)(2,1)S(1)}, u32[]{:S(2)}, u32[]{:S(2)}) collective-permute-start(bf16[512,1536]{1,0:T(8,128)(2,1)} %shard_map.220.mine_ref), channel_id=1, source_target_pairs={{0,8},{8,0},{1,9},{9,1},{2,10},{10,2},{3,11},{11,3},{4,12},{12,4},... | collective-permute-start | bytes 4718600 | tf_op jit(solution)/shard_map/ppermute | solution.py:26
  481.2 8.8 %collective-permute-start.36 = (bf16[64,2048]{1,0:T(8,128)(2,1)S(1)}, bf16[64,2048]{1,0:T(8,128)(2,1)S(1)}, u32[]{:S(2)}, u32[]{:S(2)}) collective-permute-start(bf16[64,2048]{1,0:T(8,128)(2,1)S(1)} %dynamic-slice_bitcast_fusion.1), channel_id=1, source_target_pairs={{0,16},{16,0},{1,17},{17,1},{2,18},{18,2},{3,19},{19,3},{4,20},{20... | collective-permute-start | bytes 786440 | tf_op jit(solution)/shard_map/ppermute | solution.py:30
  481.8 37.6 %all-to-all-start.5 = ((bf16[4,80,768]{2,1,0:T(8,128)(2,1)}), bf16[4,80,768]{2,1,0:T(8,128)(2,1)S(1)}, u32[]{:S(2)}, u32[]{:S(2)}) async-start(bf16[4,80,768]{2,1,0:T(8,128)(2,1)} %bitcast.15), calls=%async_computation.9 | async-start | bytes 983040 | tf_op jit(solution)/shard_map/all_to_all | solution.py:38
  490.0 21.8 %collective-permute-start.37 = (bf16[64,2048]{1,0:T(8,128)(2,1)S(1)}, bf16[64,2048]{1,0:T(8,128)(2,1)S(1)}, u32[]{:S(2)}, u32[]{:S(2)}) collective-permute-start(bf16[64,2048]{1,0:T(8,128)(2,1)S(1)} %fusion.1), channel_id=1, source_target_pairs={{0,0},{1,1},{2,8},{3,9},{4,16},{5,17},{6,24},{7,25},{8,2},{9,3},{1... | collective-permute-start | bytes 786440 | tf_op jit(solution)/shard_map/ppermute | solution.py:49
  (30 other events, 94.9 us)
Sparse Core Ops, SparseCore 0:
  9.6 56.8 all-gather.4
  73.6 46.8 all-gather.6
  126.7 44.0 reduce-scatter.4
  173.9 46.3 all-gather.8
  254.1 42.5 reduce-scatter.6
  301.1 45.2 all-gather.10
  349.2 50.8 reduce-scatter.8
  402.5 44.7 reduce-scatter.10
